TPU v7x, 1024 devices: a whole 8x8x8 slice. The times are simulated.
1024 devices in a mesh: dp: 16 (over y, core), expert: 64 (over x, z).
Axes of the slice: x: 8, y: 8, z: 8, core: 2. Of those that a mesh axis runs over, the one named last changes fastest.
Arguments:
- tokens: bfloat16 [131072, 1024], P(('dp', 'expert')), may hold values from -6 to 6
- expert_ids: int32 [131072, 2], P(('dp', 'expert')), may hold values from 0 to 63, all different within a row
- gate_weights: float32 [131072, 2], P(('dp', 'expert')), may hold values from 0.25 to 1
- replica_plan: int32 [64], replicated, may hold values from 0 to 1, as said below
- assignment: int32 [131072, 2], P(('dp', 'expert')), may hold values 0 or 1
- w_in: bfloat16 [64, 1024, 384], P('expert'), may hold values from -0.1875 to 0.1875
- w_out: bfloat16 [64, 384, 1024], P('expert'), may hold values from -0.3125 to 0.3125
- cotangent: bfloat16 [131072, 1024], P(('dp', 'expert')), may hold values from -6 to 6
Outputs:
- mixed: bfloat16 [131072, 1024], P(('dp', 'expert'))
- grad_tokens: bfloat16 [131072, 1024], P(('dp', 'expert'))
- grad_in: float32 [64, 1024, 384], P('expert', 'dp')
- grad_out: float32 [64, 384, 1024], P('expert', 'dp')
Inputs may be any that keep to these rules, and one draw needn't show every extreme that they name: `expert_ids`: each row names 2 different experts; every expert is named by some row. `replica_plan`: expert 0 always has a copy.
All inputs are finite; a program needn't handle non-finite values. No bound on the sum of `assignment` on one device may be relied on, other than what follows from the above.
Results may differ from a plain program's by a relative error of at most 0.022.
Values may be sent and summed in bfloat16 or wider, within the bound.
A program may use at most 32 MiB of HBM per device.

v0:
```python
import jax
import jax.numpy as jnp
from jax import lax
from jax.sharding import PartitionSpec as P


def partner(block, axis, apart):
    count = lax.axis_size(axis)
    route = []
    for low in range(count):
        high = low | 1 << apart
        if high != low and high < count:
            route += [(low, high), (high, low)]
    return lax.ppermute(block, axis, route)


def pair_product(form, rows, own_weight, copy_weight):
    first = jnp.einsum(form, rows[:, 0], own_weight, preferred_element_type=jnp.float32)
    second = jnp.einsum(form, rows[:, 1], copy_weight, preferred_element_type=jnp.float32)
    return jnp.stack((first, second), axis=1)


def rounded_part(form, left, right):
    product = jnp.einsum(form, left, right, preferred_element_type=jnp.float32).astype(jnp.bfloat16)
    return lax.optimization_barrier(product).astype(jnp.float32)[None]


def local(tokens, expert_ids, gate_weights, replica_plan, assignment, w_in, w_out, cotangent):
    expert_count = lax.axis_size("expert")
    tok_rows, model_width = tokens.shape
    top_count = expert_ids.shape[1]
    experts_total = replica_plan.shape[0]
    capacity = tok_rows * top_count // (2 * expert_count)
    partner_bit = expert_count.bit_length() - 2
    row_count = tok_rows * top_count
    expert_rows = expert_ids.reshape(-1)
    expert_match = (
        expert_rows[:, None] == jnp.arange(experts_total, dtype=jnp.int32)[None, :]
    ).astype(jnp.int32)
    planned = jnp.sum(expert_match * replica_plan[None, :], axis=1)
    replica_flag = assignment.reshape(-1) * planned
    partner_rows = jnp.bitwise_xor(expert_rows, 1 << partner_bit)
    target = jnp.where(replica_flag == 1, partner_rows, expert_rows)
    instance = target * 2 + replica_flag
    instance_match = (
        instance[:, None] == jnp.arange(2 * expert_count, dtype=jnp.int32)[None, :]
    ).astype(jnp.int32)
    earlier = jnp.cumsum(instance_match, axis=0) - instance_match
    row_rank = jnp.sum(earlier * instance_match, axis=1)
    keep_mask = row_rank < capacity
    slot_total = 2 * expert_count * capacity
    slot_index = jnp.where(keep_mask, instance * capacity + row_rank, slot_total)
    row_gates = gate_weights.reshape(-1) * keep_mask.astype(jnp.float32)
    buffer_shape = (expert_count, 2, capacity, model_width)
    row_ids = jnp.arange(row_count, dtype=jnp.int32)
    slot_source = (
        jnp.full((slot_total,), row_count, jnp.int32).at[slot_index].set(row_ids, mode="drop")
    )
    slot_token = slot_source // top_count
    padded_tokens = jnp.concatenate((tokens, jnp.zeros((1, model_width), tokens.dtype)), axis=0)
    padded_cotangent = jnp.concatenate(
        (cotangent, jnp.zeros((1, model_width), cotangent.dtype)), axis=0
    )
    gate_slots = jnp.concatenate((row_gates, jnp.zeros((1,), jnp.float32)), axis=0)[slot_source]
    send_rows = padded_tokens[slot_token]
    copies = partner((w_in, w_out), "expert", partner_bit)
    received = lax.all_to_all(
        send_rows.reshape(buffer_shape), "expert", split_axis=0, concat_axis=0, tiled=True
    )
    preact = pair_product("ncd,df->ncf", received, w_in[0], copies[0][0])
    hidden = jax.nn.silu(preact).astype(jnp.bfloat16)
    produced = pair_product("ncf,fd->ncd", hidden, w_out[0], copies[1][0]).astype(jnp.bfloat16)
    produced, hidden, preact, received = (produced, hidden, preact, received)
    returned_out = lax.all_to_all(
        produced, "expert", split_axis=0, concat_axis=0, tiled=True
    ).reshape(slot_total, model_width)
    picked = jnp.take(returned_out, slot_index, axis=0, mode="fill", fill_value=0)
    weighted = picked.astype(jnp.float32) * row_gates[:, None]
    mixed = jnp.sum(weighted.reshape(tok_rows, top_count, model_width), axis=1).astype(jnp.bfloat16)
    send_grads = (padded_cotangent[slot_token].astype(jnp.float32) * gate_slots[:, None]).astype(
        jnp.bfloat16
    )
    arrived = lax.all_to_all(
        send_grads.reshape(buffer_shape), "expert", split_axis=0, concat_axis=0, tiled=True
    )
    d_hidden = pair_product("ncd,fd->ncf", arrived, w_out[0], copies[1][0])
    sigmoid_pre = jax.nn.sigmoid(preact)
    d_preact = (d_hidden * sigmoid_pre * (1.0 + preact * (1.0 - sigmoid_pre))).astype(jnp.bfloat16)
    row_grads = pair_product("ncf,df->ncd", d_preact, w_in[0], copies[0][0]).astype(jnp.bfloat16)
    returned_grads = lax.all_to_all(
        row_grads, "expert", split_axis=0, concat_axis=0, tiled=True
    ).reshape(slot_total, model_width)
    picked_grads = jnp.take(returned_grads, slot_index, axis=0, mode="fill", fill_value=0)
    grad_tokens = jnp.sum(
        picked_grads.astype(jnp.float32).reshape(tok_rows, top_count, model_width), axis=1
    ).astype(jnp.bfloat16)
    own_in = rounded_part("ncd,ncf->df", received[:, 0], d_preact[:, 0])
    copy_in = rounded_part("ncd,ncf->df", received[:, 1], d_preact[:, 1])
    own_out = rounded_part("ncf,ncd->fd", hidden[:, 0], arrived[:, 0])
    copy_out = rounded_part("ncf,ncd->fd", hidden[:, 1], arrived[:, 1])
    back_in, back_out = partner(
        (copy_in.astype(jnp.bfloat16), copy_out.astype(jnp.bfloat16)), "expert", partner_bit
    )
    owner_totals = (
        lax.psum_scatter(own_in.astype(jnp.bfloat16), "dp", scatter_dimension=1, tiled=True).astype(
            jnp.float32
        ),
        lax.psum_scatter(
            back_in.astype(jnp.float32).astype(jnp.bfloat16), "dp", scatter_dimension=1, tiled=True
        ).astype(jnp.float32),
        lax.psum_scatter(
            own_out.astype(jnp.bfloat16), "dp", scatter_dimension=1, tiled=True
        ).astype(jnp.float32),
        lax.psum_scatter(
            back_out.astype(jnp.float32).astype(jnp.bfloat16), "dp", scatter_dimension=1, tiled=True
        ).astype(jnp.float32),
    )
    grad_in = owner_totals[0] + owner_totals[1]
    grad_out = owner_totals[2] + owner_totals[3]
    return (mixed, grad_tokens, grad_in, grad_out)


def solution(mesh):
    in_specs = (
        P(("dp", "expert"), None),
        P(("dp", "expert"), None),
        P(("dp", "expert"), None),
        P(),
        P(("dp", "expert"), None),
        P("expert", None, None),
        P("expert", None, None),
        P(("dp", "expert"), None),
    )
    out_specs = (
        P(("dp", "expert"), None),
        P(("dp", "expert"), None),
        P("expert", "dp", None),
        P("expert", "dp", None),
    )
    return jax.shard_map(local, mesh=mesh, in_specs=in_specs, out_specs=out_specs, check_vma=False)
```

profile of v0, /device:TPU:1, one launch (start us, length us, event | category | flops | bytes accessed | tf_op | source)
XLA Modules:
  0.0 414.8 jit_solution(18033406103719887639)
XLA Ops:
  7.2 0.8 copy.42
  8.1 0.1 reshape.171
  8.3 0.1 reshape.168
  8.4 0.8 copy.41
  9.4 0.1 reshape.167
  9.6 0.8 select_reduce_fusion
  10.5 0.2 fusion.14
  10.8 0.2 fusion.16
  11.0 1.4 scatter_custom_fusion
  12.5 1.2 gather_fusion
  13.7 1.0 reshape.172
  14.7 23.3 %all-to-all-start = ((bf16[64,2,2,1024]{3,2,1,0:T(2,128)(2,1)}), bf16[64,2,2,1024]{3,2,1,0:T(2,128)(2,1)S(1)}, u32[]{:S(2)}, u32[]{:S(2)}) async-start(bf16[64,2,2,1024]{3,2,1,0:T(2,128)(2,1)} %reshape.172), calls=%async_computation | async-start | bytes 1048576 | tf_op jit(solution)/shard_map/all_to_all | solution.py:67
  38.3 1.9 gather_fusion.2
  40.2 0.2 mul.109
  40.4 1.2 gather_fusion.1
  41.6 0.7 reshape.179
  42.3 1.2 multiply_convert_fusion
  43.5 10.8 %all-to-all-done = bf16[64,2,2,1024]{3,2,1,0:T(2,128)(2,1)S(1)} async-done(((bf16[64,2,2,1024]{3,2,1,0:T(2,128)(2,1)}), bf16[64,2,2,1024]{3,2,1,0:T(2,128)(2,1)S(1)}, u32[]{:S(2)}, u32[]{:S(2)}) %all-to-all-start) | async-done | bytes 524320 | tf_op jit(solution)/shard_map/all_to_all | solution.py:67
  54.3 8.1 %all-to-all-start.2 = ((bf16[64,2,2,1024]{3,2,1,0:T(2,128)(2,1)}), bf16[64,2,2,1024]{3,2,1,0:T(2,128)(2,1)}, u32[]{:S(2)}, u32[]{:S(2)}) async-start(bf16[64,2,2,1024]{3,2,1,0:T(2,128)(2,1)} %multiply_convert_fusion), calls=%async_computation.2 | async-start | bytes 1048576 | tf_op jit(solution)/shard_map/all_to_all | solution.py:83
  62.5 6.9 %collective-permute-start = (bf16[1,1024,384]{2,1,0:T(8,128)(2,1)S(1)}, bf16[1,1024,384]{2,1,0:T(8,128)(2,1)S(1)}, u32[]{:S(2)}, u32[]{:S(2)}) collective-permute-start(bf16[1,1024,384]{2,1,0:T(8,128)(2,1)S(1)} %copy-done), channel_id=1, source_target_pairs={{0,32},{32,0},{1,33},{33,1},{2,34},{34,2},{3,35},{35,3},{4,36},{36... | collective-permute-start | bytes 2359304 | tf_op jit(solution)/shard_map/ppermute | solution.py:14
  69.3 2.3 collective-permute-start.1
  71.7 1.4 fusion.26
  73.1 0.7 copy-done.2
  73.8 1.0 convolution_bitcast_fusion.3
  74.8 3.5 all-to-all-done.2
  78.3 1.4 fusion.25
  79.7 0.4 convolution_bitcast_fusion.1
  80.1 22.2 %collective-permute-done = bf16[1,1024,384]{2,1,0:T(8,128)(2,1)S(1)} collective-permute-done((bf16[1,1024,384]{2,1,0:T(8,128)(2,1)S(1)}, bf16[1,1024,384]{2,1,0:T(8,128)(2,1)S(1)}, u32[]{:S(2)}, u32[]{:S(2)}) %collective-permute-start) | collective-permute-done | bytes 786464 | tf_op jit(solution)/shard_map/ppermute | solution.py:14
  102.3 0.3 convolution_bitcast_fusion.2
  102.6 25.8 %collective-permute-done.1 = bf16[1,384,1024]{2,1,0:T(8,128)(2,1)S(1)} collective-permute-done((bf16[1,384,1024]{2,1,0:T(8,128)(2,1)S(1)}, bf16[1,384,1024]{2,1,0:T(8,128)(2,1)S(1)}, u32[]{:S(2)}, u32[]{:S(2)}) %collective-permute-start.1) | collective-permute-done | bytes 786464 | tf_op jit(solution)/shard_map/ppermute | solution.py:14
  128.4 0.4 convolution_bitcast_fusion
  128.8 0.8 fusion.13
  129.7 1.3 bitcast_convert_fusion.1
  131.1 1.4 bitcast_convert_fusion
  132.5 3.4 collective-permute-start.3
  135.8 19.2 %collective-permute-done.3 = bf16[1,384,1024]{2,1,0:T(8,128)(2,1)} collective-permute-done((bf16[1,384,1024]{2,1,0:T(8,128)(2,1)S(1)}, bf16[1,384,1024]{2,1,0:T(8,128)(2,1)}, u32[]{:S(2)}, u32[]{:S(2)}) %collective-permute-start.3) | collective-permute-done | bytes 786464 | tf_op jit(solution)/shard_map/ppermute | solution.py:14
  155.1 0.2 reduce-scatter.5.cloned.1.call-start
  155.3 2.3 bitcast_convert_fusion.3
  157.6 1.3 fusion.2
  159.0 0.4 fusion.3
  159.4 1.4 copy.55
  160.8 37.0 %all-to-all-start.3 = ((bf16[64,2,2,1024]{3,2,1,0:T(2,128)(2,1)}), bf16[64,2,2,1024]{3,2,1,0:T(2,128)(2,1)S(1)}, u32[]{:S(2)}, u32[]{:S(2)}) async-start(bf16[64,2,2,1024]{3,2,1,0:T(2,128)(2,1)} %copy.55), calls=%async_computation.3 | async-start | bytes 1048576 | tf_op jit(solution)/shard_map/all_to_all | solution.py:90
  197.9 0.4 bitcast_convert_fusion.2
  198.3 6.9 %collective-permute-start.2 = (bf16[1,1024,384]{2,1,0:T(8,128)(2,1)S(1)}, bf16[1,1024,384]{2,1,0:T(8,128)(2,1)}, u32[]{:S(2)}, u32[]{:S(2)}) collective-permute-start(bf16[1,1024,384]{2,1,0:T(8,128)(2,1)S(1)} %bitcast.107), channel_id=1, source_target_pairs={{0,32},{32,0},{1,33},{33,1},{2,34},{34,2},{3,35},{35,3},{4,36},{36... | collective-permute-start | bytes 2359304 | tf_op jit(solution)/shard_map/ppermute | solution.py:14
  205.2 0.3 fusion
  205.5 0.3 fusion.1
  205.9 32.1 %collective-permute-done.2 = bf16[1,1024,384]{2,1,0:T(8,128)(2,1)} collective-permute-done((bf16[1,1024,384]{2,1,0:T(8,128)(2,1)S(1)}, bf16[1,1024,384]{2,1,0:T(8,128)(2,1)}, u32[]{:S(2)}, u32[]{:S(2)}) %collective-permute-start.2) | collective-permute-done | bytes 786464 | tf_op jit(solution)/shard_map/ppermute | solution.py:14
  238.1 1.3 copy.51
  239.4 17.5 %all-to-all-start.1 = ((bf16[64,2,2,1024]{3,2,1,0:T(2,128)(2,1)}), bf16[64,2,2,1024]{3,2,1,0:T(2,128)(2,1)S(1)}, u32[]{:S(2)}, u32[]{:S(2)}) async-start(bf16[64,2,2,1024]{3,2,1,0:T(2,128)(2,1)} %copy.51), calls=%async_computation.1 | async-start | bytes 1048576 | tf_op jit(solution)/shard_map/all_to_all | solution.py:74
  257.0 0.2 reshape.176
  257.2 1.2 gather_fusion.4
  258.5 0.2 reshape.177
  258.7 2.1 reduce
  260.8 12.0 %all-to-all-done.1 = bf16[64,2,2,1024]{3,2,1,0:T(2,128)(2,1)S(1)} async-done(((bf16[64,2,2,1024]{3,2,1,0:T(2,128)(2,1)}), bf16[64,2,2,1024]{3,2,1,0:T(2,128)(2,1)S(1)}, u32[]{:S(2)}, u32[]{:S(2)}) %all-to-all-start.1) | async-done | bytes 524320 | tf_op jit(solution)/shard_map/all_to_all | solution.py:74
  272.8 0.2 reshape.173
  273.0 1.2 gather_fusion.3
  274.2 0.2 convert_multiply_fusion
  274.4 0.6 reshape.175
  275.0 2.1 reduce_sum.47
  277.1 0.5 reduce-scatter.11.cloned.1.call-done
  277.6 1.5 convert_add_fusion
  279.0 62.5 %reduce-scatter.5.cloned.1.call-done = bf16[1,64,384]{2,1,0:T(8,128)(2,1)} async-done(((bf16[1,1024,384]{2,1,0:T(8,128)(2,1)}), bf16[1,64,384]{2,1,0:T(8,128)(2,1)}) %reduce-scatter.5.cloned.1.call-update) | async-done | bytes 49168 | tf_op jit(solution)/shard_map/reduce_scatter | solution.py:105
  341.5 65.2 %reduce-scatter.7.cloned.1.call-done = bf16[1,64,384]{2,1,0:T(8,128)(2,1)} async-done(((bf16[1,1024,384]{2,1,0:T(8,128)(2,1)}), bf16[1,64,384]{2,1,0:T(8,128)(2,1)}) %reduce-scatter.7.cloned.1.call-update) | async-done | bytes 49168 | tf_op jit(solution)/shard_map/reduce_scatter | solution.py:108
  406.7 1.5 convert_add_fusion.1
  (61 shorter events, 1.4 us)
Async XLA Ops:
  7.2 5.3 %copy-start.10 = (bf16[128,1024]{1,0:T(8,128)(2,1)S(1)}, bf16[128,1024]{1,0:T(8,128)(2,1)}, u32[]{:S(2)}) copy-start(bf16[128,1024]{1,0:T(8,128)(2,1)} %param.10) | copy-start | bytes 786436
  13.7 24.3 %copy-start.12 = (f32[128,2]{0,1:T(2,128)S(1)}, f32[128,2]{0,1:T(2,128)}, u32[]{:S(2)}) copy-start(f32[128,2]{0,1:T(2,128)} %param.12) | copy-start | bytes 3076
  14.7 25.7 %copy-start.11 = (bf16[128,1024]{1,0:T(8,128)(2,1)S(1)}, bf16[128,1024]{1,0:T(8,128)(2,1)}, u32[]{:S(2)}) copy-start(bf16[128,1024]{1,0:T(8,128)(2,1)} %param.17) | copy-start | bytes 786436
  14.7 39.7 %all-to-all-start = ((bf16[64,2,2,1024]{3,2,1,0:T(2,128)(2,1)}), bf16[64,2,2,1024]{3,2,1,0:T(2,128)(2,1)S(1)}, u32[]{:S(2)}, u32[]{:S(2)}) async-start(bf16[64,2,2,1024]{3,2,1,0:T(2,128)(2,1)} %reshape.172), calls=%async_computation | async-start | bytes 1048576 | tf_op jit(solution)/shard_map/all_to_all | solution.py:67
  42.3 20.2 %copy-start = (bf16[1,1024,384]{2,1,0:T(8,128)(2,1)S(1)}, bf16[1,1024,384]{2,1,0:T(8,128)(2,1)}, u32[]{:S(2)}) copy-start(bf16[1,1024,384]{2,1,0:T(8,128)(2,1)} %param.15) | copy-start | bytes 2359300
  42.3 27.1 %copy-start.1 = (bf16[1,384,1024]{2,1,0:T(8,128)(2,1)S(1)}, bf16[1,384,1024]{2,1,0:T(8,128)(2,1)}, u32[]{:S(2)}) copy-start(bf16[1,384,1024]{2,1,0:T(8,128)(2,1)} %param.16) | copy-start | bytes 2359300
  54.3 8.1 %copy-start.4 = (bf16[64,2,2,1024]{3,2,1,0:T(2,128)(2,1)}, bf16[64,2,2,1024]{3,2,1,0:T(2,128)(2,1)S(1)}, u32[]{:S(2)}) copy-start(bf16[64,2,2,1024]{3,2,1,0:T(2,128)(2,1)S(1)} %all-to-all-done) | copy-start | bytes 1572868
  54.3 24.0 %all-to-all-start.2 = ((bf16[64,2,2,1024]{3,2,1,0:T(2,128)(2,1)}), bf16[64,2,2,1024]{3,2,1,0:T(2,128)(2,1)}, u32[]{:S(2)}, u32[]{:S(2)}) async-start(bf16[64,2,2,1024]{3,2,1,0:T(2,128)(2,1)} %multiply_convert_fusion), calls=%async_computation.2 | async-start | bytes 1048576 | tf_op jit(solution)/shard_map/all_to_all | solution.py:83
  62.4 214.7 %reduce-scatter.9.cloned.1.call-start = ((), (), s32[]{:S(2)}) async-start(), calls=%async_computation.10 | async-start | bytes 835584 | tf_op jit(solution)/shard_map/reduce_scatter | solution.py:111
  62.5 39.8 %collective-permute-start = (bf16[1,1024,384]{2,1,0:T(8,128)(2,1)S(1)}, bf16[1,1024,384]{2,1,0:T(8,128)(2,1)S(1)}, u32[]{:S(2)}, u32[]{:S(2)}) collective-permute-start(bf16[1,1024,384]{2,1,0:T(8,128)(2,1)S(1)} %copy-done), channel_id=1, source_target_pairs={{0,32},{32,0},{1,33},{33,1},{2,34},{34,2},{3,35},{35,3},{4,36},{36... | collective-permute-start | bytes 2359304 | tf_op jit(solution)/shard_map/ppermute | solution.py:14
  69.3 59.1 %collective-permute-start.1 = (bf16[1,384,1024]{2,1,0:T(8,128)(2,1)S(1)}, bf16[1,384,1024]{2,1,0:T(8,128)(2,1)S(1)}, u32[]{:S(2)}, u32[]{:S(2)}) collective-permute-start(bf16[1,384,1024]{2,1,0:T(8,128)(2,1)S(1)} %copy-done.1), channel_id=1, source_target_pairs={{0,32},{32,0},{1,33},{33,1},{2,34},{34,2},{3,35},{35,3},{4,36},{36... | collective-permute-start | bytes 2359304 | tf_op jit(solution)/shard_map/ppermute | solution.py:14
  73.1 0.7 copy-start.2
  79.7 48.8 %copy-start.3 = (bf16[64,1,2,1024]{3,2,1,0:T(2,128)(2,1)}, bf16[64,1,2,1024]{3,2,1,0:T(2,128)(2,1)S(1)}, u32[]{:S(2)}) copy-start(bf16[64,1,2,1024]{3,2,1,0:T(2,128)(2,1)S(1)} %get-tuple-element.8) | copy-start | bytes 786436
  102.3 26.5 %copy-start.9 = (f32[64,1,2,384]{3,0,2,1:T(8,128)S(1)}, f32[64,1,2,384]{3,0,2,1:T(8,128)}, u32[]{:S(2)}) copy-start(f32[64,1,2,384]{3,0,2,1:T(8,128)} %convolution_bitcast_fusion.3) | copy-start | bytes 589828
  129.7 1.3 copy-start.5
  131.0 146.6 %reduce-scatter.11.cloned.1.call-start = ((), (), s32[]{:S(2)}) async-start(), calls=%async_computation.11 | async-start | bytes 835584 | tf_op jit(solution)/shard_map/reduce_scatter | solution.py:114
  132.5 22.6 %collective-permute-start.3 = (bf16[1,384,1024]{2,1,0:T(8,128)(2,1)S(1)}, bf16[1,384,1024]{2,1,0:T(8,128)(2,1)}, u32[]{:S(2)}, u32[]{:S(2)}) collective-permute-start(bf16[1,384,1024]{2,1,0:T(8,128)(2,1)S(1)} %bitcast.108), channel_id=1, source_target_pairs={{0,32},{32,0},{1,33},{33,1},{2,34},{34,2},{3,35},{35,3},{4,36},{36... | collective-permute-start | bytes 2359304 | tf_op jit(solution)/shard_map/ppermute | solution.py:14
  155.1 186.4 %reduce-scatter.5.cloned.1.call-start = ((), (), s32[]{:S(2)}) async-start(), calls=%async_computation.8 | async-start | bytes 835584 | tf_op jit(solution)/shard_map/reduce_scatter | solution.py:105
  157.6 1.4 copy-start.7
  159.4 38.4 %copy-start.8 = (bf16[64,2,2,384]{3,0,2,1:T(8,128)(2,1)S(1)}, bf16[64,2,2,384]{3,0,2,1:T(8,128)(2,1)}, u32[]{:S(2)}) copy-start(bf16[64,2,2,384]{3,0,2,1:T(8,128)(2,1)} %get-tuple-element.11) | copy-start | bytes 589828
  160.8 44.4 %copy-start.6 = (bf16[64,2,2,384]{3,0,2,1:T(8,128)(2,1)S(1)}, bf16[64,2,2,384]{3,0,2,1:T(8,128)(2,1)}, u32[]{:S(2)}) copy-start(bf16[64,2,2,384]{3,0,2,1:T(8,128)(2,1)} %copy-done.5) | copy-start | bytes 589828
  160.8 78.6 %all-to-all-start.3 = ((bf16[64,2,2,1024]{3,2,1,0:T(2,128)(2,1)}), bf16[64,2,2,1024]{3,2,1,0:T(2,128)(2,1)S(1)}, u32[]{:S(2)}, u32[]{:S(2)}) async-start(bf16[64,2,2,1024]{3,2,1,0:T(2,128)(2,1)} %copy.55), calls=%async_computation.3 | async-start | bytes 1048576 | tf_op jit(solution)/shard_map/all_to_all | solution.py:90
  197.8 208.9 %reduce-scatter.7.cloned.1.call-start = ((), (), s32[]{:S(2)}) async-start(), calls=%async_computation.9 | async-start | bytes 835584 | tf_op jit(solution)/shard_map/reduce_scatter | solution.py:108
  198.3 39.7 %collective-permute-start.2 = (bf16[1,1024,384]{2,1,0:T(8,128)(2,1)S(1)}, bf16[1,1024,384]{2,1,0:T(8,128)(2,1)}, u32[]{:S(2)}, u32[]{:S(2)}) collective-permute-start(bf16[1,1024,384]{2,1,0:T(8,128)(2,1)S(1)} %bitcast.107), channel_id=1, source_target_pairs={{0,32},{32,0},{1,33},{33,1},{2,34},{34,2},{3,35},{35,3},{4,36},{36... | collective-permute-start | bytes 2359304 | tf_op jit(solution)/shard_map/ppermute | solution.py:14
  239.4 33.4 %all-to-all-start.1 = ((bf16[64,2,2,1024]{3,2,1,0:T(2,128)(2,1)}), bf16[64,2,2,1024]{3,2,1,0:T(2,128)(2,1)S(1)}, u32[]{:S(2)}, u32[]{:S(2)}) async-start(bf16[64,2,2,1024]{3,2,1,0:T(2,128)(2,1)} %copy.51), calls=%async_computation.1 | async-start | bytes 1048576 | tf_op jit(solution)/shard_map/all_to_all | solution.py:74
Sparse Core Ops, SparseCore 0:
  131.1 79.7 reduce-scatter.8
  214.7 62.8 reduce-scatter.10
  281.0 60.5 reduce-scatter.4
  345.1 61.5 reduce-scatter.6
where the time goes:
time: 416 us; the launch traced here: 415 us
  waiting for transfers between devices  254 us (61%)
  starting transfers between devices  106 us (25%)
  local copies, waits for them, and re-layouts  20.1 us (5%)
  between operations  14.3 us (3%)
  other arithmetic  10.9 us (3%)
  matrix products  9.67 us (2%)
    ppermute x4, waiting for transfers between devices, partner(): return lax.ppermute(block, axis, route)  99.4 us
    reduce_scatter x1, waiting for transfers between devices, local(): lax.psum_scatter(back_in.astype(jnp.float32).astype(jnp.bfloat16), 'dp',...  65.2 us
    reduce_scatter x1, waiting for transfers between devices, local(): lax.psum_scatter(own_in.astype(jnp.bfloat16), 'dp', scatter_dimension=1,...  62.5 us
    all_to_all x1, starting transfers between devices, local(): lax.all_to_all(row_grads, 'expert', split_axis=0, concat_axis=0, tiled=True)  37 us
    all_to_all x1, starting transfers between devices, local(): lax.all_to_all(send_rows.reshape(buffer_shape), 'expert', split_axis=0, c...  23.3 us
    ppermute x4, starting transfers between devices, partner(): return lax.ppermute(block, axis, route)  19.5 us
    all_to_all x1, starting transfers between devices, local(): lax.all_to_all(produced, 'expert', split_axis=0, concat_axis=0, tiled=True)  17.5 us
    all_to_all x1, waiting for transfers between devices, local(): lax.all_to_all(produced, 'expert', split_axis=0, concat_axis=0, tiled=True)  12 us
  transfers between devices with their start and end apart: 12, of which 10 were waited for; matrix products, arithmetic and copies ran while one was open for 7% of the time, Pallas kernels for 0%

commit v1 on v0

v1 whole, which is shorter than its diff:
```python
import jax
import jax.numpy as jnp
from jax import lax
from jax.sharding import PartitionSpec as P


def product(form, left, right):
    return jnp.einsum(form, left, right, preferred_element_type=jnp.float32)


def local(tokens, expert_ids, gate_weights, replica_plan, assignment, w_in, w_out, cotangent):
    expert_count = lax.axis_size("expert")
    group_count = lax.axis_size("dp")
    tok_rows, model_width = tokens.shape
    top_count = expert_ids.shape[1]
    experts_total = replica_plan.shape[0]
    capacity = tok_rows * top_count // (2 * expert_count)
    row_count = tok_rows * top_count
    expert_rows = expert_ids.reshape(-1)
    expert_match = (
        expert_rows[:, None] == jnp.arange(experts_total, dtype=jnp.int32)[None, :]
    ).astype(jnp.int32)
    planned = jnp.sum(expert_match * replica_plan[None, :], axis=1)
    instance = expert_rows * 2 + assignment.reshape(-1) * planned
    instance_match = (
        instance[:, None] == jnp.arange(2 * expert_count, dtype=jnp.int32)[None, :]
    ).astype(jnp.int32)
    earlier = jnp.cumsum(instance_match, axis=0) - instance_match
    row_rank = jnp.sum(earlier * instance_match, axis=1)
    keep_mask = row_rank < capacity
    slot_total = 2 * expert_count * capacity
    slot_index = jnp.where(keep_mask, instance * capacity + row_rank, slot_total)
    row_gates = gate_weights.reshape(-1) * keep_mask.astype(jnp.float32)
    row_ids = jnp.arange(row_count, dtype=jnp.int32)
    slot_source = (
        jnp.full((slot_total,), row_count, jnp.int32).at[slot_index].set(row_ids, mode="drop")
    )
    slot_token = slot_source // top_count
    gate_slots = jnp.concatenate((row_gates, jnp.zeros((1,), jnp.float32)), axis=0)[slot_source]
    both = jnp.concatenate((tokens, cotangent), axis=1)
    both = jnp.concatenate((both, jnp.zeros((1, 2 * model_width), both.dtype)), axis=0)[slot_token]
    scaled = (both[:, model_width:].astype(jnp.float32) * gate_slots[:, None]).astype(jnp.bfloat16)
    sent = jnp.concatenate((both[:, :model_width], scaled), axis=1)

    def exchange(rows):
        blocks = rows.reshape(expert_count, 2 * capacity, 2 * model_width)
        return lax.all_to_all(blocks, "expert", 0, 0, tiled=True).reshape(slot_total, 2 * model_width)

    got = exchange(sent)
    received, arrived = got[:, :model_width], got[:, model_width:]
    preact = product("nd,df->nf", received, w_in[0])
    gate = jax.nn.sigmoid(preact)
    hidden = (preact * gate).astype(jnp.bfloat16)
    produced = product("nf,fd->nd", hidden, w_out[0]).astype(jnp.bfloat16)
    d_hidden = product("nd,fd->nf", arrived, w_out[0])
    d_preact = (d_hidden * gate * (1.0 + preact * (1.0 - gate))).astype(jnp.bfloat16)
    row_grads = product("nf,df->nd", d_preact, w_in[0]).astype(jnp.bfloat16)
    part_in = product("nd,nf->df", received, d_preact).astype(jnp.bfloat16)
    part_out = product("nf,nd->fd", hidden, arrived).astype(jnp.bfloat16)

    back = exchange(jnp.concatenate((produced, row_grads), axis=1))
    picked = jnp.take(back, slot_index, axis=0, mode="fill", fill_value=0).astype(jnp.float32)
    weighted = picked[:, :model_width] * row_gates[:, None]
    mixed = jnp.sum(weighted.reshape(tok_rows, top_count, model_width), axis=1).astype(jnp.bfloat16)
    grad_tokens = jnp.sum(
        picked[:, model_width:].reshape(tok_rows, top_count, model_width), axis=1
    ).astype(jnp.bfloat16)

    def total(part):
        blocks = part.reshape(group_count, part.shape[0] // group_count, part.shape[1])
        blocks = lax.all_to_all(blocks, "dp", 0, 0, tiled=True)
        return jnp.sum(blocks.astype(jnp.float32), axis=0)[None]

    return (mixed, grad_tokens, total(part_in), total(part_out))


def solution(mesh):
    in_specs = (
        P(("dp", "expert"), None),
        P(("dp", "expert"), None),
        P(("dp", "expert"), None),
        P(),
        P(("dp", "expert"), None),
        P("expert", None, None),
        P("expert", None, None),
        P(("dp", "expert"), None),
    )
    out_specs = (
        P(("dp", "expert"), None),
        P(("dp", "expert"), None),
        P("expert", "dp", None),
        P("expert", "dp", None),
    )
    return jax.shard_map(local, mesh=mesh, in_specs=in_specs, out_specs=out_specs, check_vma=False)
```

time: 416 us -> 171 us (0.41)
  waiting for transfers between devices: 254 us -> 65.3 us
  starting transfers between devices: 106 us -> 21.3 us
  blocking collectives: 0 us -> 49.7 us
  between operations: 14.3 us -> 0.91 us
  local copies, waits for them, and re-layouts: 20.1 us -> 15.1 us
    reduce_scatter x4 -> x0, waiting for transfers between devices: 128 us -> none  [the longest x1 65.2 us: local(): lax.psum_scatter(back_in.astype(jnp.float32).astype(jnp.bfloat16), 'dp',...]
    ppermute x4 -> x0, waiting for transfers between devices: 99.4 us -> none  [partner(): return lax.ppermute(block, axis, route)]
    all_to_all x4 -> x3, starting transfers between devices: 85.9 us -> 21.3 us  [the longest x2 14.9 us: total(): blocks = lax.all_to_all(blocks, 'dp', 0, 0, tiled=True)]
    all_to_all x0 -> x1, blocking collectives: none -> 49.7 us  [exchange(): lax.all_to_all(blocks, 'expert', 0, 0, tiled=True)]
    all_to_all x4 -> x3, waiting for transfers between devices: 26.4 us -> 65.3 us  [the longest x2 38.6 us: total(): blocks = lax.all_to_all(blocks, 'dp', 0, 0, tiled=True)]
    ppermute x4 -> x0, starting transfers between devices: 19.5 us -> none  [partner(): return lax.ppermute(block, axis, route)]
    dot_general x12 -> x6, matrix products: 9.67 us -> 6.78 us  [product(): return jnp.einsum(form, left, right, preferred_element_type=jnp.float32)]
  transfers between devices with their start and end apart: 12 -> 3, of which waited for: 10 -> 3; matrix products, arithmetic and copies ran while one was open for 7% -> 5% of each run, Pallas kernels for 0% -> 0%
where the time goes in v1:
time: 171 us; the launch traced here: 170 us
  waiting for transfers between devices  65.3 us (38%)
  blocking collectives  49.7 us (29%)
  starting transfers between devices  21.3 us (12%)
  local copies, waits for them, and re-layouts  15.1 us (9%)
  other arithmetic  10.6 us (6%)
  matrix products  6.78 us (4%)
    all_to_all x1, blocking collectives, exchange(): lax.all_to_all(blocks, 'expert', 0, 0, tiled=True)  49.7 us
    all_to_all x2, waiting for transfers between devices, total(): blocks = lax.all_to_all(blocks, 'dp', 0, 0, tiled=True)  38.6 us
    all_to_all x1, waiting for transfers between devices, exchange(): lax.all_to_all(blocks, 'expert', 0, 0, tiled=True)  26.7 us
    all_to_all x2, starting transfers between devices, total(): blocks = lax.all_to_all(blocks, 'dp', 0, 0, tiled=True)  14.9 us
    dot_general x6, matrix products, product(): return jnp.einsum(form, left, right, preferred_element_type=jnp.float32)  6.78 us
    all_to_all x1, starting transfers between devices, exchange(): lax.all_to_all(blocks, 'expert', 0, 0, tiled=True)  6.34 us
  transfers between devices with their start and end apart: 3, of which 3 were waited for; matrix products, arithmetic and copies ran while one was open for 5% of the time, Pallas kernels for 0%

profile of v1, /device:TPU:1, one launch (start us, length us, event | category | flops | bytes accessed | tf_op | source)
XLA Modules:
  0.0 169.6 jit_solution(7819487217780051526)
XLA Ops:
  0.6 0.0 copy-start
  0.6 0.8 broadcast_multiply_fusion
  1.4 0.1 copy.23
  1.5 0.1 mul.109
  1.7 0.1 mul.105
  1.8 0.8 copy.22
  2.6 0.1 reshape.152
  2.7 0.1 reshape.150
  2.9 0.1 reshape.149
  3.0 0.8 copy.21
  3.8 0.8 copy.29
  4.6 0.1 reshape.153
  4.7 0.1 reshape.148
  4.9 0.8 select_reduce_fusion
  5.6 0.1 copy.25
  5.8 0.2 fusion.14
  6.1 0.2 fusion.16
  6.3 1.4 scatter_custom_fusion
  7.7 1.1 fusion.9
  8.8 1.4 gather_fusion
  10.2 1.9 %gather_fusion.1 = f32[256]{0:T(256)S(1)} fusion(f32[257]{0:T(512)S(1)} %pad_maximum_fusion.2, s32[1024]{0:T(1024)S(1)} %get-tuple-element.8), kind=kCustom, calls=%fused_computation.1 | custom fusion | bytes 3072 | tf_op jit(solution)/shard_map/gather | solution.py:39
  12.2 0.2 multiply_convert_fusion
  12.3 0.1 pad_maximum_fusion
  12.4 0.4 reshape.154
  12.9 49.7 %all_to_all.20 = bf16[64,4,2048]{2,1,0:T(4,128)(2,1)S(1)} all-to-all(bf16[64,4,2048]{2,1,0:T(4,128)(2,1)S(1)} %reshape.154), channel_id=1, replica_groups=mesh['dp'=16,'expert'=64] {'expert'}, dimensions={0} | all-to-all | bytes 2097152 | tf_op jit(solution)/shard_map/all_to_all | solution.py:47
  62.5 0.3 reshape.155
  62.8 0.0 copy-done
  62.8 0.4 fusion.7
  63.3 1.3 convolution_convert_fusion
  64.6 11.4 %all-to-all-start.3 = ((bf16[16,24,1024]{2,1,0:T(8,128)(2,1)}), bf16[16,24,1024]{2,1,0:T(8,128)(2,1)S(1)}, u32[]{:S(2)}, u32[]{:S(2)}) async-start(bf16[16,24,1024]{2,1,0:T(8,128)(2,1)} %bitcast.38), calls=%async_computation.3 | async-start | bytes 1572864 | tf_op jit(solution)/shard_map/all_to_all | solution.py:71
  76.0 1.6 fusion.1
  77.6 1.4 convolution_convert_fusion.1
  79.0 19.7 %all-to-all-done.3 = bf16[16,24,1024]{2,1,0:T(8,128)(2,1)S(1)} async-done(((bf16[16,24,1024]{2,1,0:T(8,128)(2,1)}), bf16[16,24,1024]{2,1,0:T(8,128)(2,1)S(1)}, u32[]{:S(2)}, u32[]{:S(2)}) %all-to-all-start.3) | async-done | bytes 786464 | tf_op jit(solution)/shard_map/all_to_all | solution.py:71
  98.7 3.5 %all-to-all-start.2 = ((bf16[16,64,384]{2,1,0:T(8,128)(2,1)}), bf16[16,64,384]{2,1,0:T(8,128)(2,1)S(1)}, u32[]{:S(2)}, u32[]{:S(2)}) async-start(bf16[16,64,384]{2,1,0:T(8,128)(2,1)} %bitcast.37), calls=%async_computation.2 | async-start | bytes 1572864 | tf_op jit(solution)/shard_map/all_to_all | solution.py:71
  102.2 0.5 convolution_convert_fusion.2
  102.6 1.6 convolution_convert_fusion.3
  104.2 0.1 pad_maximum_fusion.1
  104.3 1.2 reshape.156
  105.6 18.9 %all-to-all-done.2 = bf16[16,64,384]{2,1,0:T(8,128)(2,1)S(1)} async-done(((bf16[16,64,384]{2,1,0:T(8,128)(2,1)}), bf16[16,64,384]{2,1,0:T(8,128)(2,1)S(1)}, u32[]{:S(2)}, u32[]{:S(2)}) %all-to-all-start.2) | async-done | bytes 786464 | tf_op jit(solution)/shard_map/all_to_all | solution.py:71
  124.5 6.3 %all-to-all-start.1 = ((bf16[64,4,2048]{2,1,0:T(4,128)(2,1)}), bf16[64,4,2048]{2,1,0:T(4,128)(2,1)S(1)}, u32[]{:S(2)}, u32[]{:S(2)}) async-start(bf16[64,4,2048]{2,1,0:T(4,128)(2,1)} %reshape.156), calls=%async_computation.1 | async-start | bytes 2097152 | tf_op jit(solution)/shard_map/all_to_all | solution.py:47
  130.9 0.8 convert_reduce_fusion
  131.6 0.7 convert_reduce_fusion.1
  132.4 26.7 %all-to-all-done.1 = bf16[64,4,2048]{2,1,0:T(4,128)(2,1)S(1)} async-done(((bf16[64,4,2048]{2,1,0:T(4,128)(2,1)}), bf16[64,4,2048]{2,1,0:T(4,128)(2,1)S(1)}, u32[]{:S(2)}, u32[]{:S(2)}) %all-to-all-start.1) | async-done | bytes 1048608 | tf_op jit(solution)/shard_map/all_to_all | solution.py:47
  159.1 0.3 reshape.157
  159.3 1.4 gather_fusion.2
  160.7 0.2 select_convert_fusion
  160.9 0.2 fusion.22
  161.1 1.7 reshape.159
  162.8 0.0 copy-start.1
  162.8 1.6 reshape.158
  164.4 0.0 copy-done.1
  164.4 2.1 %reduce_sum.66 = bf16[128,1024]{1,0:T(8,128)(2,1)} reduce(f32[128,2,1024]{2,1,0:T(2,128)S(1)} %copy-done.1, f32[]{:T(128)} %constant.48.clone.1), dimensions={1}, to_apply=%region_6.7 | reduce | flops 131072 | bytes 1310724 | tf_op jit(solution)/shard_map/reduce_sum | solution.py:65
  166.4 3.2 %reduce_sum.65 = bf16[128,1024]{1,0:T(8,128)(2,1)} reduce(f32[128,2,1024]{2,1,0:T(2,128)} %reshape.158, f32[]{:T(128)} %constant.48.clone.1), dimensions={1}, to_apply=%region_5.6 | reduce | flops 131072 | bytes 1310724 | tf_op jit(solution)/shard_map/reduce_sum | solution.py:64
  (17 shorter events, 0.2 us)
Async XLA Ops:
  0.6 62.2 %copy-start = (bf16[1,1024,384]{2,1,0:T(8,128)(2,1)S(1)}, bf16[1,1024,384]{2,1,0:T(8,128)(2,1)}, u32[]{:S(2)}) copy-start(bf16[1,1024,384]{2,1,0:T(8,128)(2,1)} %param.13) | copy-start | bytes 2359300
  64.6 34.1 %all-to-all-start.3 = ((bf16[16,24,1024]{2,1,0:T(8,128)(2,1)}), bf16[16,24,1024]{2,1,0:T(8,128)(2,1)S(1)}, u32[]{:S(2)}, u32[]{:S(2)}) async-start(bf16[16,24,1024]{2,1,0:T(8,128)(2,1)} %bitcast.38), calls=%async_computation.3 | async-start | bytes 1572864 | tf_op jit(solution)/shard_map/all_to_all | solution.py:71
  98.7 25.8 %all-to-all-start.2 = ((bf16[16,64,384]{2,1,0:T(8,128)(2,1)}), bf16[16,64,384]{2,1,0:T(8,128)(2,1)S(1)}, u32[]{:S(2)}, u32[]{:S(2)}) async-start(bf16[16,64,384]{2,1,0:T(8,128)(2,1)} %bitcast.37), calls=%async_computation.2 | async-start | bytes 1572864 | tf_op jit(solution)/shard_map/all_to_all | solution.py:71
  124.5 34.6 %all-to-all-start.1 = ((bf16[64,4,2048]{2,1,0:T(4,128)(2,1)}), bf16[64,4,2048]{2,1,0:T(4,128)(2,1)S(1)}, u32[]{:S(2)}, u32[]{:S(2)}) async-start(bf16[64,4,2048]{2,1,0:T(4,128)(2,1)} %reshape.156), calls=%async_computation.1 | async-start | bytes 2097152 | tf_op jit(solution)/shard_map/all_to_all | solution.py:47
  162.8 1.6 copy-start.1

commit v2 on v1

v2 whole, which is shorter than its diff:
```python
import functools

import jax
import jax.numpy as jnp
from jax import lax
from jax.experimental import pallas as pl
from jax.experimental.pallas import tpu as pltpu
from jax.sharding import PartitionSpec as P

MESH = pl.DeviceIdType.MESH
BF16, F32, I32 = jnp.bfloat16, jnp.float32, jnp.int32
CAP = 2
SLOTS = 2 * CAP
CHUNKS = 4
BLOCK = SLOTS * CHUNKS
GROUPS = 4
STRIDE = 37


def mm(left, right, dims=((1,), (0,))):
    return lax.dot_general(left, right, (dims, ((), ())), preferred_element_type=F32)


def ones_where(mask):
    return jnp.where(mask, 1.0, 0.0).astype(BF16)


def iota(shape, dim):
    return lax.broadcasted_iota(I32, shape, dim)


def log2(n):
    return n.bit_length() - 1


def kernel(sides, n_dp, ids_ref, gates_ref, plan_ref, assign_ref, tok_hbm, cot_hbm, win_hbm, wout_hbm,
           mixed_ref, gtok_ref, gin_ref, gout_ref,
           tok, cot, win, wout, load_sem, rhs, pick, unpick, fold, unfold, spread,
           tok_send, cot_send, out_send, grad_send, tok_recv, cot_recv, out_recv, grad_recv,
           rows_in, rows_cot, pre, hid, dpre, acc0, acc1,
           part_in, part_out, pair_in, pair_out, half_in, half_out, ring_in, ring_out,
           send_sem, recv_sem, pair_send, pair_recv, ring_send, ring_recv):
    n_x, n_z = sides
    n_e = n_x * n_z
    n_y = n_dp // 2
    per = n_e // GROUPS
    rows = per * BLOCK
    live = per * SLOTS
    t, d = tok.shape
    wide = d // CHUNKS
    ff = win.shape[1]
    me, dp = lax.axis_index("expert"), lax.axis_index("dp")
    m_x, m_z = me // n_z, me % n_z
    m_y, core = dp // 2, dp % 2

    def peer(j, sign):
        off = (j * STRIDE) % n_e
        x = (m_x + sign * (off // n_z) + n_x) % n_x
        z = (m_z + sign * (off % n_z) + n_z) % n_z
        return x * n_z + z

    loads = [pltpu.make_async_copy(src, dst, load_sem.at[i]) for i, (src, dst) in enumerate(
        ((tok_hbm, tok), (cot_hbm, cot), (win_hbm.at[0], win), (wout_hbm.at[0], wout)))]
    for load in loads:
        load.start()

    barrier = pltpu.get_barrier_semaphore()

    @pl.loop(1, n_e)
    def _(j):
        pl.semaphore_signal(barrier, inc=1, device_id={"expert": peer(j, 1)}, device_id_type=MESH)

    @pl.loop(1, n_y)
    def _(j):
        pl.semaphore_signal(barrier, inc=1, device_id={"dp": ((m_y + j) % n_y) * 2 + core}, device_id_type=MESH)

    pl.semaphore_signal(barrier, inc=1, device_id={"dp": m_y * 2 + 1 - core}, device_id_type=MESH)

    plan = jnp.broadcast_to(plan_ref[...], (8, n_e)).astype(F32).astype(BF16)
    before = ones_where(iota((t, t), 0) < iota((t, t), 1))
    instances, flags, matches = [], [], []
    for k in range(2):
        ids = ids_ref[k:k + 1, :]
        match = ones_where(iota((n_e, t), 0) == ids)
        planned = mm(plan, match)[0:1, :].astype(I32)
        flag = assign_ref[k:k + 1, :] * planned
        flags.append(flag)
        matches.append(iota((2 * n_e, t), 0) == ids * 2 + flag)
    earlier = mm(ones_where(matches[0] | matches[1]), before)
    places = []
    for k in range(2):
        ids = ids_ref[k:k + 1, :]
        rank = jnp.sum(jnp.where(matches[k], earlier, 0.0), axis=0, keepdims=True).astype(I32)
        off_x = ((ids >> log2(n_z)) - m_x) & (n_x - 1)
        off_z = ((ids & (n_z - 1)) - m_z) & (n_z - 1)
        j = ((off_x * n_z + off_z) * pow(STRIDE, -1, n_e)) & (n_e - 1)
        places.append(jnp.where(rank < CAP, j * BLOCK + flags[k] * CAP + rank, -(1 << 20)))
    lanes = jnp.concatenate([places[k] + SLOTS * c for k in range(2) for c in range(CHUNKS)], axis=1)

    r, q = iota((rows, rows), 0), iota((rows, rows), 1)
    packed = ((r >> 2) & (per - 1)) * BLOCK + (r >> log2(live)) * SLOTS + (r & 3)
    fold[...] = ones_where(q == packed)
    packed = ((q >> 2) & (per - 1)) * BLOCK + (q >> log2(live)) * SLOTS + (q & 3)
    unfold[...] = ones_where(r == packed)

    def group(g):
        return pl.ds(pl.multiple_of(g * rows, rows), rows)

    def live_group(g):
        return pl.ds(pl.multiple_of(g * live, live), live)

    def send_group(g, stage, value, src, dst, sign):
        src[group(g), :] = value

        @pl.when(g == 0)
        def _():
            dst[0:BLOCK, :] = value[0:BLOCK, :]

        @pl.loop(0, per)
        def _(i):
            j = g * per + i

            @pl.when(j > 0)
            def _():
                span = pl.ds(pl.multiple_of(j * BLOCK, BLOCK), BLOCK)
                pltpu.make_async_remote_copy(
                    src_ref=src.at[span], dst_ref=dst.at[span], send_sem=send_sem.at[stage],
                    recv_sem=recv_sem.at[stage, g], device_id={"expert": peer(j, sign)}, device_id_type=MESH).start()

    def arrived(span, stage, g, dst):
        pltpu.make_async_remote_copy(
            src_ref=dst.at[span], dst_ref=dst.at[span], send_sem=send_sem.at[stage],
            recv_sem=recv_sem.at[stage, g], device_id={"expert": peer(1, 1)}, device_id_type=MESH).wait_recv()

    def wait_group(g, stage, dst):
        if per > 1:
            @pl.when(g == 0)
            def _():
                arrived(pl.ds(BLOCK, rows - BLOCK), stage, 0, dst)

        @pl.when(g > 0)
        def _():
            arrived(group(g), stage, g, dst)

    def wait_sent(stage, src, dst):
        span = pl.ds(BLOCK, (n_e - 1) * BLOCK)
        pltpu.make_async_remote_copy(
            src_ref=src.at[span], dst_ref=dst.at[span], send_sem=send_sem.at[stage],
            recv_sem=recv_sem.at[stage, 0], device_id={"expert": peer(1, 1)}, device_id_type=MESH).wait_send()

    loads[0].wait()
    for k in range(2):
        for c in range(CHUNKS):
            rhs[(k * CHUNKS + c) * t:(k * CHUNKS + c + 1) * t, :] = tok[:, c * wide:(c + 1) * wide]

    pl.semaphore_wait(barrier, n_e - 1 + n_y)

    @pl.loop(0, GROUPS)
    def _(g):
        chosen = ones_where(iota((rows, 2 * CHUNKS * t), 0) + g * rows == lanes)
        pick[group(g), :] = chosen
        send_group(g, 0, mm(chosen, rhs[...]).astype(BF16), tok_send, tok_recv, 1)

    stack_row = iota((t, t), 0)
    stack = jnp.where(stack_row == 0, places[0].astype(F32), 0.0)
    stack = jnp.where(stack_row == 1, places[1].astype(F32), stack)
    stack = jnp.where(stack_row == 2, gates_ref[0:1, :], stack)
    stack = jnp.where(stack_row == 3, gates_ref[1:2, :], stack)
    stack = stack.T
    gate_cols = [stack[:, 2 + k:3 + k] for k in range(2)]

    loads[1].wait()
    for k in range(2):
        scaled = (cot[...].astype(F32) * gate_cols[k]).astype(BF16)
        for c in range(CHUNKS):
            rhs[(k * CHUNKS + c) * t:(k * CHUNKS + c + 1) * t, :] = scaled[:, c * wide:(c + 1) * wide]

    @pl.loop(0, GROUPS)
    def _(g):
        send_group(g, 1, mm(pick[group(g), :], rhs[...]).astype(BF16), cot_send, cot_recv, 1)

    for k in range(2):
        place = stack[:, k:k + 1].astype(I32)
        for c in range(CHUNKS):
            unpick[k, c * t:(c + 1) * t, :] = ones_where(iota((t, n_e * BLOCK), 1) == place + SLOTS * c)

    per_ff = ff // n_dp
    f, q = iota((ff, 2 * ff), 0), iota((ff, 2 * ff), 1)
    shard = (f * (65536 // per_ff + 1)) >> 16
    base = (shard & 1) * ff + (shard >> 1) * (2 * per_ff) + (f - shard * per_ff)
    for h in range(2):
        spread[h] = ones_where(q == base + h * per_ff)

    def unpack(g, recv, out):
        mine = mm(fold[...], recv[group(g), :]).astype(BF16)
        for c in range(CHUNKS):
            out[live_group(g), c * wide:(c + 1) * wide] = mine[c * live:(c + 1) * live, :]

    def pack(value):
        value = value.astype(BF16)
        stacked = jnp.concatenate([value[:, c * wide:(c + 1) * wide] for c in range(CHUNKS)], axis=0)
        return mm(unfold[...], stacked).astype(BF16)

    loads[2].wait()
    loads[3].wait()

    @pl.loop(0, GROUPS)
    def _(g):
        wait_group(g, 0, tok_recv)
        unpack(g, tok_recv, rows_in)
        value = mm(rows_in[live_group(g), :], win[...])
        pre[live_group(g), :] = value
        hidden = (value * jax.nn.sigmoid(value)).astype(BF16)
        hid[live_group(g), :] = hidden
        send_group(g, 2, pack(mm(hidden, wout[...])), out_send, out_recv, -1)

    @pl.loop(0, GROUPS)
    def _(g):
        wait_group(g, 1, cot_recv)
        unpack(g, cot_recv, rows_cot)
        d_hidden = mm(rows_cot[live_group(g), :], wout[...], ((1,), (1,)))
        value = pre[live_group(g), :]
        gate = jax.nn.sigmoid(value)
        d_pre = (d_hidden * gate * (1.0 + value * (1.0 - gate))).astype(BF16)
        dpre[live_group(g), :] = d_pre
        send_group(g, 3, pack(mm(d_pre, win[...], ((1,), (1,)))), grad_send, grad_recv, -1)

    shard_in, shard_out = d // n_dp, 2 * per_ff
    total = mm(rows_in[...], dpre[...], ((0,), (0,))).astype(BF16)
    for s in range(n_dp):
        part_in[s % 2, s // 2 * shard_in:(s // 2 + 1) * shard_in, :] = total[s * shard_in:(s + 1) * shard_in, :]
    total = sum(mm(mm(hid[...], spread[h]).astype(BF16), rows_cot[:, h * d // 2:(h + 1) * d // 2], ((0,), (0,)))
                for h in range(2)).astype(BF16)
    for s in range(2):
        part_out[s] = total[s * ff:(s + 1) * ff, :]

    pair = [pltpu.make_async_remote_copy(
        src_ref=part.at[1 - core], dst_ref=other, send_sem=pair_send.at[i], recv_sem=pair_recv.at[i],
        device_id={"dp": m_y * 2 + 1 - core}, device_id_type=MESH)
        for i, (part, other) in enumerate(((part_in, pair_in), (part_out, pair_out)))]
    for copy in pair:
        copy.start()

    def gather_out(g):
        block = out_recv[group(g), :]
        return mm(unpick[0, :, group(g)], block), mm(unpick[1, :, group(g)], block)

    wait_group(0, 2, out_recv)
    acc0[...], acc1[...] = gather_out(0)

    for copy in pair:
        copy.wait_recv()
    half_in[...] = (part_in[core].astype(F32) + pair_in[...].astype(F32)).astype(BF16)
    half_out[...] = (part_out[core].astype(F32) + pair_out[...].astype(F32)).astype(BF16)

    def ring(step):
        there = (m_y + step) % n_y
        return [pltpu.make_async_remote_copy(
            src_ref=half.at[pl.ds(pl.multiple_of(there * size, 16), size)], dst_ref=got.at[step - 1],
            send_sem=ring_send.at[i], recv_sem=ring_recv.at[i],
            device_id={"dp": there * 2 + core}, device_id_type=MESH)
            for i, (half, got, size) in enumerate(((half_in, ring_in, shard_in), (half_out, ring_out, shard_out)))]

    @pl.loop(1, n_y)
    def _(step):
        for copy in ring(step):
            copy.start()

    @pl.loop(1, GROUPS)
    def _(g):
        wait_group(g, 2, out_recv)
        first, second = gather_out(g)
        acc0[...] += first
        acc1[...] += second

    for c in range(CHUNKS):
        span = slice(c * t, (c + 1) * t)
        mixed_ref[:, c * wide:(c + 1) * wide] = (
            acc0[span, :] * gate_cols[0] + acc1[span, :] * gate_cols[1]).astype(BF16)

    acc0[...] = jnp.zeros_like(acc0)

    @pl.loop(0, GROUPS)
    def _(g):
        wait_group(g, 3, grad_recv)
        acc0[...] += mm(unpick[0, :, group(g)] + unpick[1, :, group(g)], grad_recv[group(g), :])

    for c in range(CHUNKS):
        gtok_ref[:, c * wide:(c + 1) * wide] = acc0[c * t:(c + 1) * t, :].astype(BF16)

    def settle(i, half, got, wait):
        copy = pltpu.make_async_remote_copy(
            src_ref=got, dst_ref=got, send_sem=ring_send.at[i], recv_sem=ring_recv.at[i],
            device_id={"dp": m_y * 2 + 1 - core}, device_id_type=MESH)
        if wait:
            copy.wait_recv()
        else:
            copy.wait_send()

    def own(part, other, size):
        span = pl.ds(pl.multiple_of(m_y * size, 16), size)
        return part[core, span, :].astype(F32) + other[span, :].astype(F32)

    if n_y > 1:
        settle(0, half_in, ring_in, True)
    value = own(part_in, pair_in, shard_in)
    for step in range(n_y - 1):
        value += ring_in[step].astype(F32)
    gin_ref[...] = value
    if n_y > 1:
        settle(1, half_out, ring_out, True)
    value = own(part_out, pair_out, shard_out)
    for step in range(n_y - 1):
        value += ring_out[step].astype(F32)
    for h in range(2):
        gout_ref[:, h * d // 2:(h + 1) * d // 2] = value[h * per_ff:(h + 1) * per_ff, :]

    for stage, (src, dst) in enumerate(
            ((tok_send, tok_recv), (cot_send, cot_recv), (out_send, out_recv), (grad_send, grad_recv))):
        wait_sent(stage, src, dst)
    for copy in pair:
        copy.wait_send()
    if n_y > 1:
        settle(0, half_in, ring_in, False)
        settle(1, half_out, ring_out, False)


def local(sides, tokens, expert_ids, gate_weights, replica_plan, assignment, w_in, w_out, cotangent):
    n_e, n_dp = lax.axis_size("expert"), lax.axis_size("dp")
    t, d = tokens.shape
    ff = w_in.shape[2]
    n_y = n_dp // 2
    wide = d // CHUNKS
    total, live, rows = n_e * BLOCK, n_e * SLOTS, n_e // GROUPS * BLOCK
    vmem, hbm = pl.BlockSpec(memory_space=pltpu.VMEM), pl.BlockSpec(memory_space=pl.ANY)
    got_y = max(n_y - 1, 1)
    mixed, grad_tokens, grad_in, grad_out = pl.pallas_call(
        functools.partial(kernel, sides, n_dp),
        out_shape=(
            jax.ShapeDtypeStruct((t, d), BF16),
            jax.ShapeDtypeStruct((t, d), BF16),
            jax.ShapeDtypeStruct((d // n_dp, ff), F32),
            jax.ShapeDtypeStruct((ff // n_dp, d), F32),
        ),
        in_specs=[vmem] * 4 + [hbm] * 4,
        out_specs=[vmem] * 4,
        scratch_shapes=[
            pltpu.VMEM((t, d), BF16),
            pltpu.VMEM((t, d), BF16),
            pltpu.VMEM((d, ff), BF16),
            pltpu.VMEM((ff, d), BF16),
            pltpu.SemaphoreType.DMA((4,)),
            pltpu.VMEM((2 * CHUNKS * t, wide), BF16),
            pltpu.VMEM((total, 2 * CHUNKS * t), BF16),
            pltpu.VMEM((2, CHUNKS * t, total), BF16),
            pltpu.VMEM((rows, rows), BF16),
            pltpu.VMEM((rows, rows), BF16),
            pltpu.VMEM((2, ff, 2 * ff), BF16),
        ] + [pltpu.VMEM((total, wide), BF16)] * 8 + [
            pltpu.VMEM((live, d), BF16),
            pltpu.VMEM((live, d), BF16),
            pltpu.VMEM((live, ff), F32),
            pltpu.VMEM((live, ff), BF16),
            pltpu.VMEM((live, ff), BF16),
            pltpu.VMEM((CHUNKS * t, wide), F32),
            pltpu.VMEM((CHUNKS * t, wide), F32),
            pltpu.VMEM((2, d // 2, ff), BF16),
            pltpu.VMEM((2, ff, d // 2), BF16),
            pltpu.VMEM((d // 2, ff), BF16),
            pltpu.VMEM((ff, d // 2), BF16),
            pltpu.VMEM((d // 2, ff), BF16),
            pltpu.VMEM((ff, d // 2), BF16),
            pltpu.VMEM((got_y, d // n_dp, ff), BF16),
            pltpu.VMEM((got_y, 2 * ff // n_dp, d // 2), BF16),
            pltpu.SemaphoreType.DMA((4,)),
            pltpu.SemaphoreType.DMA((4, GROUPS)),
            pltpu.SemaphoreType.DMA((2,)),
            pltpu.SemaphoreType.DMA((2,)),
            pltpu.SemaphoreType.DMA((2,)),
            pltpu.SemaphoreType.DMA((2,)),
        ],
        compiler_params=pltpu.CompilerParams(
            collective_id=0, has_side_effects=True, vmem_limit_bytes=48 << 20),
    )(expert_ids.T, gate_weights.T, replica_plan[None], assignment.T, tokens, cotangent, w_in, w_out)
    return mixed, grad_tokens, grad_in[None], grad_out[None]


def solution(mesh):
    count = mesh.shape["expert"]
    n_x = 1 << (log2(count) // 2)
    in_specs = (
        P(("dp", "expert"), None),
        P(("dp", "expert"), None),
        P(("dp", "expert"), None),
        P(),
        P(("dp", "expert"), None),
        P("expert", None, None),
        P("expert", None, None),
        P(("dp", "expert"), None),
    )
    out_specs = (
        P(("dp", "expert"), None),
        P(("dp", "expert"), None),
        P("expert", "dp", None),
        P("expert", "dp", None),
    )
    return jax.shard_map(functools.partial(local, (n_x, count // n_x)), mesh=mesh, in_specs=in_specs,
                         out_specs=out_specs, check_vma=False)
```

time: 171 us -> 88.2 us (0.52)
  the two profiles are of different devices: /device:TPU:1 before, /device:TPU:5 now
where the time goes in v2:
time: 88.2 us; the launch traced here: 87.9 us
  Pallas kernels  79.7 us (90%)
  local copies, waits for them, and re-layouts  7.53 us (9%)
    pallas_call x1, Pallas kernels, local(): pl.pallas_call(functools.partial(kernel, sides, n_dp), out_shape=(jax.Sha...  79.7 us
    unnamed x20, local copies, waits for them, and re-layouts  7.53 us

profile of v2, /device:TPU:5, one launch (start us, length us, event | category | flops | bytes accessed | tf_op | source)
XLA Modules:
  0.0 87.9 jit_solution(10050803459602028997)
XLA Ops:
  0.6 0.0 copy-start.5
  0.6 0.0 copy-start.6
  0.7 0.0 copy-start.4
  0.7 0.0 copy-start.7
  0.7 0.6 copy-done.5
  1.3 0.0 copy-done.6
  1.3 0.0 copy-done.4
  1.3 0.0 copy-done.7
  1.3 0.0 copy-start
  1.4 1.1 %copy-done = bf16[1,1024,384]{2,1,0:T(8,128)(2,1)S(1)} copy-done((bf16[1,1024,384]{2,1,0:T(8,128)(2,1)S(1)}, bf16[1,1024,384]{2,1,0:T(8,128)(2,1)}, u32[]{:S(2)}) %copy-start) | copy-done | bytes 786456
  2.5 0.0 copy-start.1
  2.5 1.1 %copy-done.1 = bf16[1,384,1024]{2,1,0:T(8,128)(2,1)S(1)} copy-done((bf16[1,384,1024]{2,1,0:T(8,128)(2,1)S(1)}, bf16[1,384,1024]{2,1,0:T(8,128)(2,1)}, u32[]{:S(2)}) %copy-start.1) | copy-done | bytes 786456
  3.6 0.0 copy-start.2
  3.6 0.9 %copy-done.2 = bf16[128,1024]{1,0:T(8,128)(2,1)S(1)} copy-done((bf16[128,1024]{1,0:T(8,128)(2,1)S(1)}, bf16[128,1024]{1,0:T(8,128)(2,1)}, u32[]{:S(2)}) %copy-start.2) | copy-done | bytes 262168
  4.6 0.0 copy-start.3
  4.6 0.9 %copy-done.3 = bf16[128,1024]{1,0:T(8,128)(2,1)S(1)} copy-done((bf16[128,1024]{1,0:T(8,128)(2,1)S(1)}, bf16[128,1024]{1,0:T(8,128)(2,1)}, u32[]{:S(2)}) %copy-start.3) | copy-done | bytes 262168
  5.5 79.7 %shard_map.111 = (bf16[128,1024]{1,0:T(8,128)(2,1)S(1)}, bf16[128,1024]{1,0:T(8,128)(2,1)S(1)}, f32[64,384]{1,0:T(8,128)S(1)}, f32[24,1024]{1,0:T(8,128)S(1)}) custom-call(s32[2,128]{1,0:T(2,128)S(1)} %bitcast.8, f32[2,128]{1,0:T(2,128)S(1)} %bitcast.9, s32[1,64]{1,0:T(1,128)S(1)} %bitcast.11, s32[2,128]{1,0:T(2,128)S(1)} %bitcast.10, ...), custom_call_target="tpu_custom_call" | custom-call | tf_op jit(solution)/shard_map/pallas_call | solution.py:337
  85.2 0.7 copy.16
  85.9 0.7 copy.17
  86.7 0.6 copy.18
  87.3 0.6 copy.19
Async XLA Ops:
  0.6 0.7 copy-start.5
  0.6 0.7 copy-start.6
  0.7 0.7 copy-start.4
  0.7 0.7 copy-start.7
  1.3 1.1 %copy-start = (bf16[1,1024,384]{2,1,0:T(8,128)(2,1)S(1)}, bf16[1,1024,384]{2,1,0:T(8,128)(2,1)}, u32[]{:S(2)}) copy-start(bf16[1,1024,384]{2,1,0:T(8,128)(2,1)} %win_hbm.1) | copy-start | bytes 2359300
  2.5 1.1 %copy-start.1 = (bf16[1,384,1024]{2,1,0:T(8,128)(2,1)S(1)}, bf16[1,384,1024]{2,1,0:T(8,128)(2,1)}, u32[]{:S(2)}) copy-start(bf16[1,384,1024]{2,1,0:T(8,128)(2,1)} %wout_hbm.1) | copy-start | bytes 2359300
  3.6 0.9 %copy-start.2 = (bf16[128,1024]{1,0:T(8,128)(2,1)S(1)}, bf16[128,1024]{1,0:T(8,128)(2,1)}, u32[]{:S(2)}) copy-start(bf16[128,1024]{1,0:T(8,128)(2,1)} %tok_hbm.1) | copy-start | bytes 786436
  4.6 0.9 %copy-start.3 = (bf16[128,1024]{1,0:T(8,128)(2,1)S(1)}, bf16[128,1024]{1,0:T(8,128)(2,1)}, u32[]{:S(2)}) copy-start(bf16[128,1024]{1,0:T(8,128)(2,1)} %cot_hbm.1) | copy-start | bytes 786436

commit v3 on v2

--- a/solution.py
+++ b/solution.py
@@ -34,7 +34,8 @@
 
 
 def kernel(sides, n_dp, ids_ref, gates_ref, plan_ref, assign_ref, tok_hbm, cot_hbm, win_hbm, wout_hbm,
-           mixed_ref, gtok_ref, gin_ref, gout_ref,
+           mixed_hbm, gtok_hbm, gin_hbm, gout_hbm,
+           mixed_ref, gtok_ref, gin_ref, gout_ref, store_sem,
            tok, cot, win, wout, load_sem, rhs, pick, unpick, fold, unfold, spread,
            tok_send, cot_send, out_send, grad_send, tok_recv, cot_recv, out_recv, grad_recv,
            rows_in, rows_cot, pre, hid, dpre, acc0, acc1,
@@ -59,6 +60,8 @@
         z = (m_z + sign * (off % n_z) + n_z) % n_z
         return x * n_z + z
 
+    stores = [pltpu.make_async_copy(src, dst, store_sem.at[i]) for i, (src, dst) in enumerate(
+        ((mixed_ref, mixed_hbm), (gtok_ref, gtok_hbm), (gin_ref, gin_hbm), (gout_ref, gout_hbm)))]
     loads = [pltpu.make_async_copy(src, dst, load_sem.at[i]) for i, (src, dst) in enumerate(
         ((tok_hbm, tok), (cot_hbm, cot), (win_hbm.at[0], win), (wout_hbm.at[0], wout)))]
     for load in loads:
@@ -70,9 +73,9 @@
     def _(j):
         pl.semaphore_signal(barrier, inc=1, device_id={"expert": peer(j, 1)}, device_id_type=MESH)
 
-    @pl.loop(1, n_y)
-    def _(j):
-        pl.semaphore_signal(barrier, inc=1, device_id={"dp": ((m_y + j) % n_y) * 2 + core}, device_id_type=MESH)
+    along_y = {1: (), 2: (1,)}.get(n_y, (1, n_y - 1))
+    for step in along_y:
+        pl.semaphore_signal(barrier, inc=1, device_id={"dp": ((m_y + step) % n_y) * 2 + core}, device_id_type=MESH)
 
     pl.semaphore_signal(barrier, inc=1, device_id={"dp": m_y * 2 + 1 - core}, device_id_type=MESH)
 
@@ -153,7 +156,7 @@
         for c in range(CHUNKS):
             rhs[(k * CHUNKS + c) * t:(k * CHUNKS + c + 1) * t, :] = tok[:, c * wide:(c + 1) * wide]
 
-    pl.semaphore_wait(barrier, n_e - 1 + n_y)
+    pl.semaphore_wait(barrier, n_e + len(along_y))
 
     @pl.loop(0, GROUPS)
     def _(g):
@@ -214,16 +217,23 @@
         hid[live_group(g), :] = hidden
         send_group(g, 2, pack(mm(hidden, wout[...])), out_send, out_recv, -1)
 
-    @pl.loop(0, GROUPS)
-    def _(g):
+    def backward(g):
         wait_group(g, 1, cot_recv)
         unpack(g, cot_recv, rows_cot)
         d_hidden = mm(rows_cot[live_group(g), :], wout[...], ((1,), (1,)))
         value = pre[live_group(g), :]
         gate = jax.nn.sigmoid(value)
-        d_pre = (d_hidden * gate * (1.0 + value * (1.0 - gate))).astype(BF16)
-        dpre[live_group(g), :] = d_pre
-        send_group(g, 3, pack(mm(d_pre, win[...], ((1,), (1,)))), grad_send, grad_recv, -1)
+        dpre[live_group(g), :] = (d_hidden * gate * (1.0 + value * (1.0 - gate))).astype(BF16)
+
+    def send_grads(g):
+        send_group(g, 3, pack(mm(dpre[live_group(g), :], win[...], ((1,), (1,)))), grad_send, grad_recv, -1)
+
+    @pl.loop(0, GROUPS - 1)
+    def _(g):
+        backward(g)
+        send_grads(g)
+
+    backward(GROUPS - 1)
 
     shard_in, shard_out = d // n_dp, 2 * per_ff
     total = mm(rows_in[...], dpre[...], ((0,), (0,))).astype(BF16)
@@ -241,88 +251,119 @@
     for copy in pair:
         copy.start()
 
-    def gather_out(g):
-        block = out_recv[group(g), :]
-        return mm(unpick[0, :, group(g)], block), mm(unpick[1, :, group(g)], block)
-
-    wait_group(0, 2, out_recv)
-    acc0[...], acc1[...] = gather_out(0)
+    send_grads(GROUPS - 1)
 
     for copy in pair:
         copy.wait_recv()
     half_in[...] = (part_in[core].astype(F32) + pair_in[...].astype(F32)).astype(BF16)
     half_out[...] = (part_out[core].astype(F32) + pair_out[...].astype(F32)).astype(BF16)
 
-    def ring(step):
-        there = (m_y + step) % n_y
-        return [pltpu.make_async_remote_copy(
-            src_ref=half.at[pl.ds(pl.multiple_of(there * size, 16), size)], dst_ref=got.at[step - 1],
-            send_sem=ring_send.at[i], recv_sem=ring_recv.at[i],
-            device_id={"dp": there * 2 + core}, device_id_type=MESH)
-            for i, (half, got, size) in enumerate(((half_in, ring_in, shard_in), (half_out, ring_out, shard_out)))]
-
-    @pl.loop(1, n_y)
-    def _(step):
-        for copy in ring(step):
-            copy.start()
-
-    @pl.loop(1, GROUPS)
-    def _(g):
+    hops = n_y // 2
+    chains = ((1, 1, half_in, ring_in.at[0], shard_in), (2, -1, half_in, ring_in.at[1], shard_in),
+              (2, 1, half_out, ring_out.at[0], shard_out), (1, -1, half_out, ring_out.at[1], shard_out))
+
+    def hop(i, step):
+        first, way, half, got, size = chains[i]
+        there = (m_y + way * (hops + 1 - step) + n_y) % n_y
+        mine = half.at[pl.ds(pl.multiple_of(there * size, 16), size)]
+        if step > first:
+            mine, term = got.at[step - 2], mine
+            travel(i, step - 1, mine, got).wait_recv()
+            mine[...] = (mine[...].astype(F32) + term[...].astype(F32)).astype(BF16)
+        return travel(i, step, mine, got)
+
+    def travel(i, step, src, got):
+        return pltpu.make_async_remote_copy(
+            src_ref=src, dst_ref=got.at[step - 1], send_sem=ring_send.at[i, step - 1],
+            recv_sem=ring_recv.at[i, step - 1],
+            device_id={"dp": ((m_y + chains[i][1] + n_y) % n_y) * 2 + core}, device_id_type=MESH)
+
+    sent = []
+
+    def advance(turn):
+        for i in (0, 3, 1, 2):
+            step = chains[i][0] + turn
+            if step <= hops:
+                sent.append(hop(i, step))
+                sent[-1].start()
+
+    acc0[...] = jnp.zeros_like(acc0)
+    acc1[...] = jnp.zeros_like(acc1)
+
+    def gather_out(g):
         wait_group(g, 2, out_recv)
-        first, second = gather_out(g)
-        acc0[...] += first
-        acc1[...] += second
+        block = out_recv[group(g), :]
+        acc0[...] += mm(unpick[0, :, group(g)], block)
+        acc1[...] += mm(unpick[1, :, group(g)], block)
+
+    turns = max(hops, 1)
+    for turn in range(max(turns, GROUPS)):
+        if turn < turns:
+            advance(turn)
+        if turn < GROUPS:
+            gather_out(turn)
 
     for c in range(CHUNKS):
         span = slice(c * t, (c + 1) * t)
         mixed_ref[:, c * wide:(c + 1) * wide] = (
             acc0[span, :] * gate_cols[0] + acc1[span, :] * gate_cols[1]).astype(BF16)
 
+    stores[0].start()
     acc0[...] = jnp.zeros_like(acc0)
 
-    @pl.loop(0, GROUPS)
-    def _(g):
+    def gather_grads(g):
         wait_group(g, 3, grad_recv)
         acc0[...] += mm(unpick[0, :, group(g)] + unpick[1, :, group(g)], grad_recv[group(g), :])
 
+    def complete(part, other, ends):
+        size = chains[ends[0]][4]
+        span = pl.ds(pl.multiple_of(m_y * size, 16), size)
+        value = part[core, span, :].astype(F32) + other[span, :].astype(F32)
+        for i in ends:
+            if chains[i][0] <= hops:
+                got = chains[i][3]
+                travel(i, hops, got.at[hops - 1], got).wait_recv()
+                value += got[hops - 1].astype(F32)
+        return value
+
+    gin_ref[...] = complete(part_in, pair_in, (0, 1))
+    stores[2].start()
+    value = complete(part_out, pair_out, (2, 3))
+    for h in range(2):
+        gout_ref[:, h * d // 2:(h + 1) * d // 2] = value[h * per_ff:(h + 1) * per_ff, :]
+    stores[3].start()
+
+    @pl.loop(0, GROUPS - 1)
+    def _(g):
+        gather_grads(g)
+
+    gather_grads(GROUPS - 1)
     for c in range(CHUNKS):
         gtok_ref[:, c * wide:(c + 1) * wide] = acc0[c * t:(c + 1) * t, :].astype(BF16)
-
-    def settle(i, half, got, wait):
-        copy = pltpu.make_async_remote_copy(
-            src_ref=got, dst_ref=got, send_sem=ring_send.at[i], recv_sem=ring_recv.at[i],
-            device_id={"dp": m_y * 2 + 1 - core}, device_id_type=MESH)
-        if wait:
-            copy.wait_recv()
-        else:
-            copy.wait_send()
-
-    def own(part, other, size):
-        span = pl.ds(pl.multiple_of(m_y * size, 16), size)
-        return part[core, span, :].astype(F32) + other[span, :].astype(F32)
-
-    if n_y > 1:
-        settle(0, half_in, ring_in, True)
-    value = own(part_in, pair_in, shard_in)
-    for step in range(n_y - 1):
-        value += ring_in[step].astype(F32)
-    gin_ref[...] = value
-    if n_y > 1:
-        settle(1, half_out, ring_out, True)
-    value = own(part_out, pair_out, shard_out)
-    for step in range(n_y - 1):
-        value += ring_out[step].astype(F32)
-    for h in range(2):
-        gout_ref[:, h * d // 2:(h + 1) * d // 2] = value[h * per_ff:(h + 1) * per_ff, :]
+    stores[1].start()
 
     for stage, (src, dst) in enumerate(
             ((tok_send, tok_recv), (cot_send, cot_recv), (out_send, out_recv), (grad_send, grad_recv))):
         wait_sent(stage, src, dst)
     for copy in pair:
         copy.wait_send()
-    if n_y > 1:
-        settle(0, half_in, ring_in, False)
-        settle(1, half_out, ring_out, False)
+    for copy in sent:
+        copy.wait_send()
+    for store in stores:
+        store.wait()
+
+
+def through(*refs):
+    sources, targets, held, sem = refs[:4], refs[4:8], refs[8:12], refs[12]
+    ins = [pltpu.make_async_copy(sources[i], held[i], sem.at[0, i]) for i in range(4)]
+    outs = [pltpu.make_async_copy(held[i], targets[i], sem.at[1, i]) for i in range(4)]
+    for copy in ins:
+        copy.start()
+    for i in range(4):
+        ins[i].wait()
+        outs[i].start()
+    for copy in outs:
+        copy.wait()
 
 
 def local(sides, tokens, expert_ids, gate_weights, replica_plan, assignment, w_in, w_out, cotangent):
@@ -333,8 +374,8 @@
     wide = d // CHUNKS
     total, live, rows = n_e * BLOCK, n_e * SLOTS, n_e // GROUPS * BLOCK
     vmem, hbm = pl.BlockSpec(memory_space=pltpu.VMEM), pl.BlockSpec(memory_space=pl.ANY)
-    got_y = max(n_y - 1, 1)
-    mixed, grad_tokens, grad_in, grad_out = pl.pallas_call(
+    hops = max(n_y // 2, 1)
+    results = pl.pallas_call(
         functools.partial(kernel, sides, n_dp),
         out_shape=(
             jax.ShapeDtypeStruct((t, d), BF16),
@@ -343,8 +384,13 @@
             jax.ShapeDtypeStruct((ff // n_dp, d), F32),
         ),
         in_specs=[vmem] * 4 + [hbm] * 4,
-        out_specs=[vmem] * 4,
+        out_specs=[hbm] * 4,
         scratch_shapes=[
+            pltpu.VMEM((t, d), BF16),
+            pltpu.VMEM((t, d), BF16),
+            pltpu.VMEM((d // n_dp, ff), F32),
+            pltpu.VMEM((ff // n_dp, d), F32),
+            pltpu.SemaphoreType.DMA((4,)),
             pltpu.VMEM((t, d), BF16),
             pltpu.VMEM((t, d), BF16),
             pltpu.VMEM((d, ff), BF16),
@@ -370,19 +416,27 @@
             pltpu.VMEM((ff, d // 2), BF16),
             pltpu.VMEM((d // 2, ff), BF16),
             pltpu.VMEM((ff, d // 2), BF16),
-            pltpu.VMEM((got_y, d // n_dp, ff), BF16),
-            pltpu.VMEM((got_y, 2 * ff // n_dp, d // 2), BF16),
+            pltpu.VMEM((2, hops, d // n_dp, ff), BF16),
+            pltpu.VMEM((2, hops, 2 * ff // n_dp, d // 2), BF16),
             pltpu.SemaphoreType.DMA((4,)),
             pltpu.SemaphoreType.DMA((4, GROUPS)),
             pltpu.SemaphoreType.DMA((2,)),
             pltpu.SemaphoreType.DMA((2,)),
-            pltpu.SemaphoreType.DMA((2,)),
-            pltpu.SemaphoreType.DMA((2,)),
+            pltpu.SemaphoreType.DMA((4, hops)),
+            pltpu.SemaphoreType.DMA((4, hops)),
         ],
         compiler_params=pltpu.CompilerParams(
-            collective_id=0, has_side_effects=True, vmem_limit_bytes=48 << 20),
+            collective_id=0, has_side_effects=True, vmem_limit_bytes=63 << 20),
     )(expert_ids.T, gate_weights.T, replica_plan[None], assignment.T, tokens, cotangent, w_in, w_out)
-    return mixed, grad_tokens, grad_in[None], grad_out[None]
+    results = pl.pallas_call(
+        through,
+        out_shape=tuple(jax.ShapeDtypeStruct(r.shape, r.dtype) for r in results),
+        in_specs=[hbm] * 4,
+        out_specs=[hbm] * 4,
+        scratch_shapes=[pltpu.VMEM(r.shape, r.dtype) for r in results] + [pltpu.SemaphoreType.DMA((2, 4))],
+        compiler_params=pltpu.CompilerParams(vmem_limit_bytes=63 << 20),
+    )(*results)
+    return results[0], results[1], results[2][None], results[3][None]
 
 
 def solution(mesh):

time: 88.2 us -> 76.8 us (0.87)
  the two profiles are of different devices: /device:TPU:5 before, /device:TPU:1 now
where the time goes in v3:
time: 76.8 us; the launch traced here: 76.6 us
  Pallas kernels  76 us (99%)
    pallas_call x1, Pallas kernels, local(): pl.pallas_call(functools.partial(kernel, sides, n_dp), out_shape=(jax.Sha...  74.1 us
    pallas_call x1, Pallas kernels, local(): pl.pallas_call(through, out_shape=tuple((jax.ShapeDtypeStruct(r.shape, r....  1.87 us

profile of v3, /device:TPU:1, one launch (start us, length us, event | category | flops | bytes accessed | tf_op | source)
XLA Modules:
  0.0 76.6 jit_solution(10495867842686120344)
XLA Ops:
  0.6 74.1 %shard_map.111 = (bf16[128,1024]{1,0:T(8,128)(2,1)}, bf16[128,1024]{1,0:T(8,128)(2,1)}, f32[64,384]{1,0:T(8,128)}, f32[24,1024]{1,0:T(8,128)}) custom-call(s32[2,128]{1,0:T(2,128)} %bitcast.6, f32[2,128]{1,0:T(2,128)} %bitcast.7, s32[1,64]{1,0:T(1,128)} %bitcast.9, s32[2,128]{1,0:T(2,128)} %bitcast.8, bf16[128,1024]{1,0:T(8,128)(2,1)} %tok_hbm.1, ...), custom_call_target="tpu_custom_call" | custom-call | tf_op jit(solution)/shard_map/pallas_call | solution.py:378
  74.7 1.9 %shard_map.112 = (bf16[128,1024]{1,0:T(8,128)(2,1)}, bf16[128,1024]{1,0:T(8,128)(2,1)}, f32[64,384]{1,0:T(8,128)}, f32[24,1024]{1,0:T(8,128)}) custom-call(bf16[128,1024]{1,0:T(8,128)(2,1)} %get-tuple-element.12.refs_0_, bf16[128,1024]{1,0:T(8,128)(2,1)} %get-tuple-element.13.refs_1_, f32[64,384]{1,0:T(8,128)} %get-tuple-element.14.refs_2_, ...), custom_call_target="tpu_custom_call" | custom-call | tf_op jit(solution)/shard_map/pallas_call | solution.py:431

commit v4 on v3

--- a/solution.py
+++ b/solution.py
@@ -34,8 +34,7 @@
 
 
 def kernel(sides, n_dp, ids_ref, gates_ref, plan_ref, assign_ref, tok_hbm, cot_hbm, win_hbm, wout_hbm,
-           mixed_hbm, gtok_hbm, gin_hbm, gout_hbm,
-           mixed_ref, gtok_ref, gin_ref, gout_ref, store_sem,
+           mixed_ref, gtok_ref, gin_ref, gout_ref,
            tok, cot, win, wout, load_sem, rhs, pick, unpick, fold, unfold, spread,
            tok_send, cot_send, out_send, grad_send, tok_recv, cot_recv, out_recv, grad_recv,
            rows_in, rows_cot, pre, hid, dpre, acc0, acc1,
@@ -54,14 +53,12 @@
     m_x, m_z = me // n_z, me % n_z
     m_y, core = dp // 2, dp % 2
 
-    def peer(j, sign):
-        off = (j * STRIDE) % n_e
-        x = (m_x + sign * (off // n_z) + n_x) % n_x
-        z = (m_z + sign * (off % n_z) + n_z) % n_z
+    def peer(g, i, sign):
+        off = lax.rem(g * (per * STRIDE % n_e) + i * STRIDE % n_e, n_e)
+        x = lax.rem(m_x + sign * lax.div(off, n_z) + n_x, n_x)
+        z = lax.rem(m_z + sign * lax.rem(off, n_z) + n_z, n_z)
         return x * n_z + z
 
-    stores = [pltpu.make_async_copy(src, dst, store_sem.at[i]) for i, (src, dst) in enumerate(
-        ((mixed_ref, mixed_hbm), (gtok_ref, gtok_hbm), (gin_ref, gin_hbm), (gout_ref, gout_hbm)))]
     loads = [pltpu.make_async_copy(src, dst, load_sem.at[i]) for i, (src, dst) in enumerate(
         ((tok_hbm, tok), (cot_hbm, cot), (win_hbm.at[0], win), (wout_hbm.at[0], wout)))]
     for load in loads:
@@ -69,9 +66,11 @@
 
     barrier = pltpu.get_barrier_semaphore()
 
-    @pl.loop(1, n_e)
-    def _(j):
-        pl.semaphore_signal(barrier, inc=1, device_id={"expert": peer(j, 1)}, device_id_type=MESH)
+    for x in range(n_x):
+        for z in range(n_z):
+            if x or z:
+                there = lax.rem(m_x + x, n_x) * n_z + lax.rem(m_z + z, n_z)
+                pl.semaphore_signal(barrier, inc=1, device_id={"expert": there}, device_id_type=MESH)
 
     along_y = {1: (), 2: (1,)}.get(n_y, (1, n_y - 1))
     for step in along_y:
@@ -119,21 +118,24 @@
         def _():
             dst[0:BLOCK, :] = value[0:BLOCK, :]
 
-        @pl.loop(0, per)
-        def _(i):
-            j = g * per + i
-
-            @pl.when(j > 0)
-            def _():
-                span = pl.ds(pl.multiple_of(j * BLOCK, BLOCK), BLOCK)
-                pltpu.make_async_remote_copy(
-                    src_ref=src.at[span], dst_ref=dst.at[span], send_sem=send_sem.at[stage],
-                    recv_sem=recv_sem.at[stage, g], device_id={"expert": peer(j, sign)}, device_id_type=MESH).start()
+        def start(i):
+            span = pl.ds(pl.multiple_of((g * per + i) * BLOCK, BLOCK), BLOCK)
+            pltpu.make_async_remote_copy(
+                src_ref=src.at[span], dst_ref=dst.at[span], send_sem=send_sem.at[stage],
+                recv_sem=recv_sem.at[stage, g], device_id={"expert": peer(g, i, sign)},
+                device_id_type=MESH).start()
+
+        @pl.when(g > 0)
+        def _():
+            start(0)
+
+        for i in range(1, per):
+            start(i)
 
     def arrived(span, stage, g, dst):
         pltpu.make_async_remote_copy(
             src_ref=dst.at[span], dst_ref=dst.at[span], send_sem=send_sem.at[stage],
-            recv_sem=recv_sem.at[stage, g], device_id={"expert": peer(1, 1)}, device_id_type=MESH).wait_recv()
+            recv_sem=recv_sem.at[stage, g], device_id={"expert": peer(0, 1, 1)}, device_id_type=MESH).wait_recv()
 
     def wait_group(g, stage, dst):
         if per > 1:
@@ -149,7 +151,7 @@
         span = pl.ds(BLOCK, (n_e - 1) * BLOCK)
         pltpu.make_async_remote_copy(
             src_ref=src.at[span], dst_ref=dst.at[span], send_sem=send_sem.at[stage],
-            recv_sem=recv_sem.at[stage, 0], device_id={"expert": peer(1, 1)}, device_id_type=MESH).wait_send()
+            recv_sem=recv_sem.at[stage, 0], device_id={"expert": peer(0, 1, 1)}, device_id_type=MESH).wait_send()
 
     loads[0].wait()
     for k in range(2):
@@ -308,7 +310,6 @@
         mixed_ref[:, c * wide:(c + 1) * wide] = (
             acc0[span, :] * gate_cols[0] + acc1[span, :] * gate_cols[1]).astype(BF16)
 
-    stores[0].start()
     acc0[...] = jnp.zeros_like(acc0)
 
     def gather_grads(g):
@@ -327,11 +328,9 @@
         return value
 
     gin_ref[...] = complete(part_in, pair_in, (0, 1))
-    stores[2].start()
     value = complete(part_out, pair_out, (2, 3))
     for h in range(2):
         gout_ref[:, h * d // 2:(h + 1) * d // 2] = value[h * per_ff:(h + 1) * per_ff, :]
-    stores[3].start()
 
     @pl.loop(0, GROUPS - 1)
     def _(g):
@@ -340,7 +339,6 @@
     gather_grads(GROUPS - 1)
     for c in range(CHUNKS):
         gtok_ref[:, c * wide:(c + 1) * wide] = acc0[c * t:(c + 1) * t, :].astype(BF16)
-    stores[1].start()
 
     for stage, (src, dst) in enumerate(
             ((tok_send, tok_recv), (cot_send, cot_recv), (out_send, out_recv), (grad_send, grad_recv))):
@@ -349,20 +347,13 @@
         copy.wait_send()
     for copy in sent:
         copy.wait_send()
-    for store in stores:
-        store.wait()
 
 
 def through(*refs):
-    sources, targets, held, sem = refs[:4], refs[4:8], refs[8:12], refs[12]
-    ins = [pltpu.make_async_copy(sources[i], held[i], sem.at[0, i]) for i in range(4)]
-    outs = [pltpu.make_async_copy(held[i], targets[i], sem.at[1, i]) for i in range(4)]
-    for copy in ins:
+    copies = [pltpu.make_async_copy(refs[i], refs[4 + i], refs[8].at[i]) for i in range(4)]
+    for copy in copies:
         copy.start()
-    for i in range(4):
-        ins[i].wait()
-        outs[i].start()
-    for copy in outs:
+    for copy in copies:
         copy.wait()
 
 
@@ -378,19 +369,13 @@
     results = pl.pallas_call(
         functools.partial(kernel, sides, n_dp),
         out_shape=(
-            jax.ShapeDtypeStruct((t, d), BF16),
-            jax.ShapeDtypeStruct((t, d), BF16),
-            jax.ShapeDtypeStruct((d // n_dp, ff), F32),
-            jax.ShapeDtypeStruct((ff // n_dp, d), F32),
-        ),
-        in_specs=[vmem] * 4 + [hbm] * 4,
-        out_specs=[hbm] * 4,
-        scratch_shapes=[
             pltpu.VMEM((t, d), BF16),
             pltpu.VMEM((t, d), BF16),
             pltpu.VMEM((d // n_dp, ff), F32),
             pltpu.VMEM((ff // n_dp, d), F32),
-            pltpu.SemaphoreType.DMA((4,)),
+        ),
+        in_specs=[vmem] * 4 + [hbm] * 4,
+        scratch_shapes=[
             pltpu.VMEM((t, d), BF16),
             pltpu.VMEM((t, d), BF16),
             pltpu.VMEM((d, ff), BF16),
@@ -426,15 +411,15 @@
             pltpu.SemaphoreType.DMA((4, hops)),
         ],
         compiler_params=pltpu.CompilerParams(
-            collective_id=0, has_side_effects=True, vmem_limit_bytes=63 << 20),
+            collective_id=0, has_side_effects=True, vmem_limit_bytes=62 << 20),
     )(expert_ids.T, gate_weights.T, replica_plan[None], assignment.T, tokens, cotangent, w_in, w_out)
     results = pl.pallas_call(
         through,
         out_shape=tuple(jax.ShapeDtypeStruct(r.shape, r.dtype) for r in results),
-        in_specs=[hbm] * 4,
+        in_specs=[vmem] * 4,
         out_specs=[hbm] * 4,
-        scratch_shapes=[pltpu.VMEM(r.shape, r.dtype) for r in results] + [pltpu.SemaphoreType.DMA((2, 4))],
-        compiler_params=pltpu.CompilerParams(vmem_limit_bytes=63 << 20),
+        scratch_shapes=[pltpu.SemaphoreType.DMA((4,))],
+        compiler_params=pltpu.CompilerParams(vmem_limit_bytes=16 << 20),
     )(*results)
     return results[0], results[1], results[2][None], results[3][None]
 

time: 76.8 us -> 73.8 us (0.961)
  Pallas kernels: 76 us -> 73 us
    pallas_call x1, Pallas kernels: 74.1 us -> 72.1 us  [local(): pl.pallas_call(functools.partial(kernel, sides, n_dp), out_shape=(pltpu.V...]
    pallas_call x1, Pallas kernels: 1.87 us -> 0.88 us  [local(): pl.pallas_call(through, out_shape=tuple((jax.ShapeDtypeStruct(r.shape, r....]
where the time goes in v4:
time: 73.8 us; the launch traced here: 73.6 us
  Pallas kernels  73 us (99%)
    pallas_call x1, Pallas kernels, local(): pl.pallas_call(functools.partial(kernel, sides, n_dp), out_shape=(pltpu.V...  72.1 us

profile of v4, /device:TPU:1, one launch (start us, length us, event | category | flops | bytes accessed | tf_op | source)
XLA Modules:
  0.0 73.6 jit_solution(3393142964208260285)
XLA Ops:
  0.6 72.1 %shard_map.111 = (bf16[128,1024]{1,0:T(8,128)(2,1)S(1)}, bf16[128,1024]{1,0:T(8,128)(2,1)S(1)}, f32[64,384]{1,0:T(8,128)S(1)}, f32[24,1024]{1,0:T(8,128)S(1)}) custom-call(s32[2,128]{1,0:T(2,128)} %bitcast.6, f32[2,128]{1,0:T(2,128)} %bitcast.7, s32[1,64]{1,0:T(1,128)} %bitcast.9, s32[2,128]{1,0:T(2,128)} %bitcast.8, bf16[128,1024]{1,0:T(8,128)(2,1)} %tok_hbm.1, ...), custom_call_target="tpu_custom_call" | custom-call | tf_op jit(solution)/shard_map/pallas_call | solution.py:369
  72.7 0.9 %shard_map.112 = (bf16[128,1024]{1,0:T(8,128)(2,1)}, bf16[128,1024]{1,0:T(8,128)(2,1)}, f32[64,384]{1,0:T(8,128)}, f32[24,1024]{1,0:T(8,128)}) custom-call(bf16[128,1024]{1,0:T(8,128)(2,1)S(1)} %get-tuple-element.12.refs_0_, bf16[128,1024]{1,0:T(8,128)(2,1)S(1)} %get-tuple-element.13.refs_1_, f32[64,384]{1,0:T(8,128)S(1)} %get-tuple-element.14.refs_2_, ...), custom_call_target="tpu_custom_call" | custom-call | tf_op jit(solution)/shard_map/pallas_call | solution.py:416

commit v5 on v4

--- a/solution.py
+++ b/solution.py
@@ -33,9 +33,9 @@
     return n.bit_length() - 1
 
 
-def kernel(sides, n_dp, ids_ref, gates_ref, plan_ref, assign_ref, tok_hbm, cot_hbm, win_hbm, wout_hbm,
+def kernel(sides, n_dp, ids_hbm, gates_hbm, plan_hbm, assign_hbm, tok_hbm, cot_hbm, win_hbm, wout_hbm,
            mixed_ref, gtok_ref, gin_ref, gout_ref,
-           tok, cot, win, wout, load_sem, rhs, pick, unpick, fold, unfold, spread,
+           ids_ref, gates_ref, plan_ref, assign_ref, tok, cot, win, wout, load_sem, rhs, pick, unpick, fold, unfold, spread,
            tok_send, cot_send, out_send, grad_send, tok_recv, cot_recv, out_recv, grad_recv,
            rows_in, rows_cot, pre, hid, dpre, acc0, acc1,
            part_in, part_out, pair_in, pair_out, half_in, half_out, ring_in, ring_out,
@@ -60,8 +60,9 @@
         return x * n_z + z
 
     loads = [pltpu.make_async_copy(src, dst, load_sem.at[i]) for i, (src, dst) in enumerate(
-        ((tok_hbm, tok), (cot_hbm, cot), (win_hbm.at[0], win), (wout_hbm.at[0], wout)))]
-    for load in loads:
+        ((tok_hbm, tok), (cot_hbm, cot), (win_hbm.at[0], win), (wout_hbm.at[0], wout), (ids_hbm, ids_ref),
+         (gates_hbm, gates_ref), (plan_hbm, plan_ref), (assign_hbm, assign_ref)))]
+    for load in loads[4:] + loads[:4]:
         load.start()
 
     barrier = pltpu.get_barrier_semaphore()
@@ -78,6 +79,8 @@
 
     pl.semaphore_signal(barrier, inc=1, device_id={"dp": m_y * 2 + 1 - core}, device_id_type=MESH)
 
+    for load in loads[4:]:
+        load.wait()
     plan = jnp.broadcast_to(plan_ref[...], (8, n_e)).astype(F32).astype(BF16)
     before = ones_where(iota((t, t), 0) < iota((t, t), 1))
     instances, flags, matches = [], [], []
@@ -374,13 +377,17 @@
             pltpu.VMEM((d // n_dp, ff), F32),
             pltpu.VMEM((ff // n_dp, d), F32),
         ),
-        in_specs=[vmem] * 4 + [hbm] * 4,
+        in_specs=[hbm] * 8,
         scratch_shapes=[
+            pltpu.VMEM((2, t), I32),
+            pltpu.VMEM((2, t), F32),
+            pltpu.VMEM((1, n_e), I32),
+            pltpu.VMEM((2, t), I32),
             pltpu.VMEM((t, d), BF16),
             pltpu.VMEM((t, d), BF16),
             pltpu.VMEM((d, ff), BF16),
             pltpu.VMEM((ff, d), BF16),
-            pltpu.SemaphoreType.DMA((4,)),
+            pltpu.SemaphoreType.DMA((8,)),
             pltpu.VMEM((2 * CHUNKS * t, wide), BF16),
             pltpu.VMEM((total, 2 * CHUNKS * t), BF16),
             pltpu.VMEM((2, CHUNKS * t, total), BF16),

time: 73.8 us -> 73.2 us (level)
  no operation moved by 1% of the time
where the time goes in v5:
time: 73.2 us; the launch traced here: 73.1 us
  Pallas kernels  72.4 us (99%)
    pallas_call x1, Pallas kernels, local(): pl.pallas_call(functools.partial(kernel, sides, n_dp), out_shape=(pltpu.V...  71.5 us

profile of v5, /device:TPU:1, one launch (start us, length us, event | category | flops | bytes accessed | tf_op | source)
XLA Modules:
  0.0 73.1 jit_solution(15466479552237075084)
XLA Ops:
  0.6 71.5 %shard_map.111 = (bf16[128,1024]{1,0:T(8,128)(2,1)S(1)}, bf16[128,1024]{1,0:T(8,128)(2,1)S(1)}, f32[64,384]{1,0:T(8,128)S(1)}, f32[24,1024]{1,0:T(8,128)S(1)}) custom-call(s32[2,128]{1,0:T(2,128)} %bitcast.6, f32[2,128]{1,0:T(2,128)} %bitcast.7, s32[1,64]{1,0:T(1,128)} %bitcast.9, s32[2,128]{1,0:T(2,128)} %bitcast.8, bf16[128,1024]{1,0:T(8,128)(2,1)} %tok_hbm.1, ...), custom_call_target="tpu_custom_call" | custom-call | tf_op jit(solution)/shard_map/pallas_call | solution.py:372
  72.2 0.9 %shard_map.112 = (bf16[128,1024]{1,0:T(8,128)(2,1)}, bf16[128,1024]{1,0:T(8,128)(2,1)}, f32[64,384]{1,0:T(8,128)}, f32[24,1024]{1,0:T(8,128)}) custom-call(bf16[128,1024]{1,0:T(8,128)(2,1)S(1)} %get-tuple-element.12.refs_0_, bf16[128,1024]{1,0:T(8,128)(2,1)S(1)} %get-tuple-element.13.refs_1_, f32[64,384]{1,0:T(8,128)S(1)} %get-tuple-element.14.refs_2_, ...), custom_call_target="tpu_custom_call" | custom-call | tf_op jit(solution)/shard_map/pallas_call | solution.py:423
